TPU v7x, 512 devices: a whole 4x8x8 slice. The times are simulated.
512 devices in a mesh: ctx: 64 (over x, z, core), head: 8 (over y).
Axes of the slice: x: 4, y: 8, z: 8, core: 2. Of those that a mesh axis runs over, the one named last changes fastest.
Arguments:
- q_lin: bfloat16 [32768, 4096], P('ctx', 'head'), may hold values from -6 to 6
- k_lin: bfloat16 [32768, 4096], P('ctx', 'head'), may hold values from -6 to 6
- v_lin: bfloat16 [32768, 4096], P('ctx', 'head'), may hold values from -30 to 30
- out_gate: bfloat16 [32768, 4096], P('ctx', 'head'), may hold values from -6 to 6
- grad_out: bfloat16 [32768, 4096], P('ctx', 'head'), may hold values from -6 to 6
- log_decay: float32 [32768, 32], P('ctx', 'head'), may hold values from -1 to 0
- norm_gain: float32 [4096], P('head'), may hold values from 0.1 to 1.9
Outputs:
- grad_query: bfloat16 [32768, 4096], P('ctx', 'head')
- grad_key: bfloat16 [32768, 4096], P('ctx', 'head')
- grad_value: bfloat16 [32768, 4096], P('ctx', 'head')
- grad_gate: bfloat16 [32768, 4096], P('ctx', 'head')
All inputs are finite; a program needn't handle non-finite values.
Results may differ from a plain program's by a relative error of at most 0.007.
Values sent between devices are 32-bit elements; how exact they have to be, the bound alone decides.
A program may use at most 128 MiB of HBM per device.

v0:
```python
import jax
import jax.numpy as jnp
from jax import lax
from jax.sharding import PartitionSpec as P

BLOCK = 512


def carried_in(part, axis, combine, identity, reverse):
    count = lax.axis_size(axis)
    place = lax.axis_index(axis)
    ahead = count - 1 - place if reverse else place
    gathered = jax.tree.map(lambda a: lax.all_gather(a, axis), part)
    state = jax.tree.map(lambda a, e: jnp.zeros_like(a) + jnp.asarray(e, a.dtype), part, identity)

    def one(hop, state):
        source = count - 1 - hop if reverse else hop
        return combine(
            state, jax.tree.map(lambda a: lax.dynamic_index_in_dim(a, source, 0, False), gathered)
        )

    return lax.fori_loop(0, ahead, one, state)


def decay_blocks(cumul, lower_tri):
    trans = jnp.swapaxes(cumul, 1, 2)
    diff = trans[:, :, :, None] - trans[:, :, None, :]
    return jnp.where(lower_tri, jnp.exp(jnp.where(lower_tri, diff, 0.0)), 0.0)


def chain_forward(decays, local_terms):
    carried = jnp.zeros_like(local_terms[0])
    states = [carried]
    carried = decays[0][:, None, None] * carried + local_terms[0]
    return (jnp.stack(states), carried)


def chain_reverse(decays, local_terms):
    carried = jnp.zeros_like(local_terms[0])
    states = [carried] * local_terms.shape[0]
    for block_idx in reversed(range(local_terms.shape[0])):
        states[block_idx] = carried
        carried = decays[block_idx][:, None, None] * carried + local_terms[block_idx]
    return (jnp.stack(states), carried)


def join_forward(earlier_part, later_part):
    return (
        earlier_part[0] * later_part[0],
        later_part[0][:, None, None] * earlier_part[1] + later_part[1],
    )


def join_reverse(earlier_part, later_part):
    return (
        later_part[0] * earlier_part[0],
        later_part[1] + later_part[0][:, None, None] * earlier_part[1],
    )


def local(q_lin, k_lin, v_lin, out_gate, grad_out, log_decay, norm_gain):
    tok_rows = q_lin.shape[0]
    heads_here = log_decay.shape[1]
    head_dim = q_lin.shape[1] // heads_here
    num_blocks = tok_rows // BLOCK
    block_shape = (num_blocks, BLOCK, heads_here, head_dim)
    queries = q_lin.reshape(block_shape)
    keyed = k_lin.reshape(block_shape)
    valued = v_lin.reshape(block_shape)
    cumul = jnp.cumsum(log_decay.reshape(num_blocks, BLOCK, heads_here), axis=1)
    totals = cumul[:, -1, :]
    tail_decay = jnp.exp(totals[:, None, :] - cumul)
    head_decay = jnp.exp(cumul)
    lower_tri = jnp.arange(BLOCK)[:, None] >= jnp.arange(BLOCK)[None, :]
    decays = decay_blocks(cumul, lower_tri)
    block_decay = jnp.exp(totals)
    device_decay = jnp.prod(block_decay, axis=0)
    identity = (
        jnp.ones((heads_here,), jnp.float32),
        jnp.zeros((heads_here, head_dim, head_dim), jnp.float32),
    )
    weighted_key = (keyed * tail_decay[..., None]).astype(jnp.bfloat16)
    block_state = jnp.einsum(
        "nbhk,nbhv->nhkv", weighted_key, valued, preferred_element_type=jnp.float32
    )
    local_in, device_state = chain_forward(block_decay, block_state)
    prefix = carried_in((device_decay, device_state), "ctx", join_forward, identity, False)
    before = jnp.exp(jnp.cumsum(totals, axis=0) - totals)
    entering_b = (local_in + before[:, :, None, None] * prefix[1][None]).astype(jnp.bfloat16)
    scores = jnp.einsum("nthd,nshd->nhts", queries, keyed, preferred_element_type=jnp.float32)
    forward_decay_weights = (scores * decays).astype(jnp.bfloat16)
    attended = jnp.einsum(
        "nhts,nshd->nthd", forward_decay_weights, valued, preferred_element_type=jnp.float32
    )
    attended = attended + head_decay[..., None] * jnp.einsum(
        "nthk,nhkv->nthv", queries, entering_b, preferred_element_type=jnp.float32
    )
    attended = attended.reshape(tok_rows, heads_here * head_dim)
    gate_sig = jax.nn.sigmoid(out_gate.astype(jnp.float32))
    grad_o = grad_out.astype(jnp.float32)
    grad_normed = grad_o * gate_sig * norm_gain[None, :]
    features = heads_here * head_dim * lax.axis_size("head")
    row_squares = jnp.sum(attended * attended, axis=1)
    row_inner = jnp.sum(grad_normed * attended, axis=1)
    squares, inner_sum = lax.psum((row_squares, row_inner), "head")
    rms_flat = lax.rsqrt(squares / features + 1e-05)
    coef_flat = rms_flat**3 * inner_sum / features
    rms_inv = rms_flat[:, None]
    grad_gate = (
        grad_o * attended * rms_inv * norm_gain[None, :] * gate_sig * (1.0 - gate_sig)
    ).astype(jnp.bfloat16)
    grad_attn = (rms_inv * grad_normed - attended * coef_flat[:, None]).astype(jnp.bfloat16)
    grad_blk = grad_attn.reshape(block_shape)
    reverse_decay_weights = (
        jnp.einsum("nthd,nshd->nhts", grad_blk, valued, preferred_element_type=jnp.float32) * decays
    ).astype(jnp.bfloat16)
    weighted_query = (queries * head_decay[..., None]).astype(jnp.bfloat16)
    block_reverse = jnp.einsum(
        "nbhk,nbhv->nhkv", weighted_query, grad_blk, preferred_element_type=jnp.float32
    )
    local_out, device_reverse = chain_reverse(block_decay, block_reverse)
    suffix = carried_in((device_decay, device_reverse), "ctx", join_reverse, identity, True)
    after = jnp.exp(jnp.sum(totals, axis=0)[None, :] - jnp.cumsum(totals, axis=0))
    leaving_b = (local_out + after[:, :, None, None] * suffix[1][None]).astype(jnp.bfloat16)
    query_gradient = jnp.einsum(
        "nhts,nshd->nthd", reverse_decay_weights, keyed, preferred_element_type=jnp.float32
    )
    query_gradient = query_gradient + head_decay[..., None] * jnp.einsum(
        "nthv,nhkv->nthk", grad_blk, entering_b, preferred_element_type=jnp.float32
    )
    key_gradient = jnp.einsum(
        "nhts,nthd->nshd", reverse_decay_weights, queries, preferred_element_type=jnp.float32
    )
    key_gradient = key_gradient + tail_decay[..., None] * jnp.einsum(
        "nshv,nhkv->nshk", valued, leaving_b, preferred_element_type=jnp.float32
    )
    value_gradient = jnp.einsum(
        "nhts,nthd->nshd", forward_decay_weights, grad_blk, preferred_element_type=jnp.float32
    )
    value_gradient = value_gradient + tail_decay[..., None] * jnp.einsum(
        "nshk,nhkv->nshv", keyed, leaving_b, preferred_element_type=jnp.float32
    )
    grad_query = query_gradient.reshape(tok_rows, heads_here * head_dim).astype(jnp.bfloat16)
    grad_key = key_gradient.reshape(tok_rows, heads_here * head_dim).astype(jnp.bfloat16)
    grad_value = value_gradient.reshape(tok_rows, heads_here * head_dim).astype(jnp.bfloat16)
    return (grad_query, grad_key, grad_value, grad_gate)


def solution(mesh):
    return jax.shard_map(
        local,
        mesh=mesh,
        in_specs=(
            P("ctx", "head"),
            P("ctx", "head"),
            P("ctx", "head"),
            P("ctx", "head"),
            P("ctx", "head"),
            P("ctx", "head"),
            P("head"),
        ),
        out_specs=(P("ctx", "head"), P("ctx", "head"), P("ctx", "head"), P("ctx", "head")),
        check_vma=False,
    )
```

profile of v0, /device:TPU:1, one launch (start us, length us, event | category | flops | bytes accessed | tf_op | source)
XLA Modules:
  0.0 395.3 jit_solution(18245956354886973788)
XLA Ops:
  8.1 1.2 reduce-window.6
  10.1 1.3 copy.138
  13.0 46.4 %all-gather = f32[64,1,4]{2,1,0:T(1,128)S(1)} all-gather(f32[1,1,4]{2,1,0:T(1,128)S(1)} %get-tuple-element.175), channel_id=2, replica_groups=mesh['ctx'=64,'head'=8] {'ctx'}, dimensions={0}, use_global_device_ids=true | all-gather | bytes 1040 | tf_op jit(solution)/shard_map/all_gather | solution.py:13
  59.5 1.5 multiply_convert_fusion.1
  61.0 1.3 copy-done.1
  63.2 61.4 %all-gather.6.cloned.1.call-done = f32[256,128,128]{2,1,0:T(8,128)} async-done(((f32[4,128,128]{2,1,0:T(8,128)}), f32[256,128,128]{2,1,0:T(8,128)}) %all-gather.6.cloned.1.call-update) | async-done | bytes 16777232 | tf_op jit(solution)/shard_map/all_gather | solution.py:13
  124.6 1.1 while.26
  124.7 1.1 bitcast_add_fusion.7
  126.6 1.7 multiply_reduce_fusion
  128.2 13.2 %all-reduce = (f32[512]{0:T(512)S(1)}, f32[512]{0:T(512)S(1)}) all-reduce(f32[512]{0:T(512)S(1)} %multiply_reduce_fusion, f32[512]{0:T(512)S(1)} %get-tuple-element.178), channel_id=1, replica_groups=mesh['ctx'=64,'head'=8] {'head'}, use_global_device_ids=true, to_apply=%region_7.8 | all-reduce | flops 1024 | bytes 8192 | tf_op jit(solution)/shard_map/psum | solution.py:105
  141.5 2.6 fusion.16
  145.4 1.5 multiply_convert_fusion
  147.8 2.8 fusion.10
  150.5 2.0 copy.101
  152.6 2.6 convolution_bitcast_fusion.1
  155.7 158.8 %all-gather.8.cloned.1.call-done = f32[256,128,128]{2,1,0:T(8,128)} async-done(((f32[4,128,128]{2,1,0:T(8,128)}), f32[256,128,128]{2,1,0:T(8,128)}) %all-gather.8.cloned.1.call-update) | async-done | bytes 16777232 | tf_op jit(solution)/shard_map/all_gather | solution.py:13
  314.5 68.2 %while.27 = (s32[]{:T(128)}, f32[4,128,128]{2,1,0:T(8,128)S(1)}, s32[]{:T(128)}, f32[64,4,128,128]{3,2,1,0:T(8,128)}, f32[64,4]{1,0:T(8,128)S(1)}, /*index=5*/s32[]{:T(128)}, s32[]{:T(128)}, s32[]{:T(128)}, s32[]{:T(128)}) while((s32[]{:T(128)}, f32[4,128,128]{2,1,0:T(8,128)S(1)}, s32[]{:T(128)}, f32[64,4,128,128]{3,2,1,0:T(8,128)}, ...), condition=%wide.region_9.10_spmd, body=%wide.region_8.9_spmd.sunk | while | flops 131078 | bytes 786635 | solution.py:22
  314.6 1.1 bitcast_add_fusion.8
  315.7 1.1 bitcast_add_fusion.8
  316.8 1.1 bitcast_add_fusion.8
  317.9 1.1 bitcast_add_fusion.8
  319.0 1.1 bitcast_add_fusion.8
  320.1 1.1 bitcast_add_fusion.8
  321.2 1.1 bitcast_add_fusion.8
  322.3 1.1 bitcast_add_fusion.8
  323.4 1.1 bitcast_add_fusion.8
  324.5 1.1 bitcast_add_fusion.8
  325.6 1.1 bitcast_add_fusion.8
  326.7 1.1 bitcast_add_fusion.8
  327.8 1.1 bitcast_add_fusion.8
  330.0 1.1 bitcast_add_fusion.8
  333.3 1.1 bitcast_add_fusion.8
  336.6 1.1 bitcast_add_fusion.8
  339.9 1.1 bitcast_add_fusion.8
  344.3 1.1 bitcast_add_fusion.8
  347.6 1.1 bitcast_add_fusion.8
  350.9 1.1 bitcast_add_fusion.8
  354.2 1.1 bitcast_add_fusion.8
  357.5 1.1 bitcast_add_fusion.8
  360.8 1.1 bitcast_add_fusion.8
  365.2 1.1 bitcast_add_fusion.8
  368.5 1.1 bitcast_add_fusion.8
  371.8 1.1 bitcast_add_fusion.8
  375.1 1.1 bitcast_add_fusion.8
  378.4 1.1 bitcast_add_fusion.8
  381.7 1.1 bitcast_add_fusion.8
  382.8 2.3 fusion.8
  385.0 2.0 copy.103
  (157 shorter events, 44.4 us)
Async XLA Ops:
  7.2 4.2 %copy-start = (bf16[512,512]{1,0:T(8,128)(2,1)S(1)}, bf16[512,512]{1,0:T(8,128)(2,1)}, u32[]{:S(2)}) copy-start(bf16[512,512]{1,0:T(8,128)(2,1)} %param.13) | copy-start | bytes 1572868
  7.2 52.3 %copy-start.9 = (bf16[512,512]{1,0:T(8,128)(2,1)S(1)}, bf16[512,512]{1,0:T(8,128)(2,1)}, u32[]{:S(2)}) copy-start(bf16[512,512]{1,0:T(8,128)(2,1)} %param.12) | copy-start | bytes 1572868
  7.2 5.6 %copy-start.10 = (bf16[512,512]{1,0:T(8,128)(2,1)S(1)}, bf16[512,512]{1,0:T(8,128)(2,1)}, u32[]{:S(2)}) copy-start(bf16[512,512]{1,0:T(8,128)(2,1)} %param.11) | copy-start | bytes 1572868
  7.2 117.4 %all-gather.6.cloned.1.call-start = ((), (), s32[]{:S(2)}) async-start(), calls=%async_computation | async-start | bytes 17039360 | tf_op jit(solution)/shard_map/all_gather | solution.py:13
  11.4 1.2 copy-start.7
  12.4 302.1 %all-gather.8.cloned.1.call-start = ((), (), s32[]{:S(2)}) async-start(), calls=%async_computation.1 | async-start | bytes 17039360 | tf_op jit(solution)/shard_map/all_gather | solution.py:13
  59.4 1.6 copy-start.11
  61.0 1.3 copy-start.1
  124.6 1.9 copy-start.13
  126.6 18.8 %copy-start.12 = (pred[512,512]{1,0:T(8,128)(4,1)S(1)}, pred[512,512]{1,0:T(8,128)(4,1)}, u32[]{:S(2)}) copy-start(pred[512,512]{1,0:T(8,128)(4,1)} %copy-done.11) | copy-start | bytes 786436
  144.3 1.1 copy-start.5
  145.4 1.6 copy-start.8
  147.0 3.6 copy-start.3
  147.0 5.6 %copy-start.2 = (bf16[4,512,512]{2,1,0:T(8,128)(2,1)S(1)}, bf16[4,512,512]{2,1,0:T(8,128)(2,1)}, u32[]{:S(2)}) copy-start(bf16[4,512,512]{2,1,0:T(8,128)(2,1)} %copy-done.1) | copy-start | bytes 6291460
  152.6 2.6 copy-start.4
  155.2 227.5 %copy-start.6 = (f32[1,512,4,128]{1,3,2,0:T(8,128)S(1)}, f32[1,512,4,128]{1,3,2,0:T(8,128)}, u32[]{:S(2)}) copy-start(f32[1,512,4,128]{1,3,2,0:T(8,128)} %convolution_bitcast_fusion.1) | copy-start | bytes 3145732
Sparse Core Ops, SparseCore 0:
  12.6 112.0 all-gather.5
  145.5 168.9 all-gather.7
where the time goes:
time: 398 us; the launch traced here: 395 us
  waiting for transfers between devices  220 us (55%)
  other arithmetic  72.7 us (18%)
  blocking collectives  59.6 us (15%)
  matrix products  15.6 us (4%)
  between operations  14.4 us (4%)
  local copies, waits for them, and re-layouts  10.8 us (3%)
    all_gather x2, waiting for transfers between devices, carried_in(): gathered = jax.tree.map(lambda a: lax.all_gather(a, axis), part)  220 us
    add x62, other arithmetic, join_reverse(): later_part[1] + later_part[0][:, None, None] * earlier_part[1]  65.8 us
    all_gather x1, blocking collectives, carried_in(): gathered = jax.tree.map(lambda a: lax.all_gather(a, axis), part)  46.4 us
    psum x1, blocking collectives, local(): squares, inner_sum = lax.psum((row_squares, row_inner), 'head')  13.2 us
  transfers between devices with their start and end apart: 2, of which 2 were waited for; matrix products, arithmetic and copies ran while one was open for 3% of the time, Pallas kernels for 0%

commit v1 on v0

v1 whole, which is shorter than its diff:
```python
import functools

import jax
import jax.numpy as jnp
from jax import lax
from jax.experimental import pallas as pl
from jax.experimental.pallas import tpu as pltpu
from jax.sharding import PartitionSpec as P

BLOCK = 512
DH = 128
HEADS = 4
HALF = HEADS // 2 * DH
TILE = 256
NX = 4
NZ = 8
F32 = jnp.float32
BF16 = jnp.bfloat16
MESH = pl.DeviceIdType.MESH


def nn(a, b):
    return jnp.dot(a, b, preferred_element_type=F32)


def nt(a, b):
    return lax.dot_general(a, b, (((1,), (1,)), ((), ())), preferred_element_type=F32)


def lane_cumsum(x):
    place = lax.broadcasted_iota(jnp.int32, x.shape, 1)
    step = 1
    while step < x.shape[1]:
        x = x + jnp.where(place >= step, pltpu.roll(x, step, 1), 0.0)
        step *= 2
    return x


def columns(row):
    return jnp.broadcast_to(row, (DH, row.shape[1])).T


def kernel(
    nx, nz, nh,
    q_hbm, k_hbm, v_hbm, gate_hbm, gout_hbm, ld_hbm, gain_hbm,
    dq_hbm, dk_hbm, dv_hbm, dg_hbm,
    q, k, v, gate, gout, ld, gain,
    dq, dk, dv, dg,
    a_row, ea_row, tail_row, ea_col, tail_col,
    qt, wqt, wq, wk, wv, mask, fw, att, gn, gg, gb, dki, dvi,
    f_own, f_par, f_chip, f_zin, f_xout, f_xin, f_back, f_ent, f_pair, f_state,
    r_own, r_par, r_chip, r_zin, r_xout, r_xin, r_back, r_ent, r_pair, r_state,
    y_out, y_in,
    local_sem, send_sem, recv_sem,
):
    me, head = lax.axis_index("ctx"), lax.axis_index("head")
    core, z, x = me % 2, (me // 2) % nz, me // (2 * nz)
    rows = HALF // nz

    def at(xx, zz, cc):
        return ((xx * nz + zz) * 2 + cc, head)

    partner = at(x, z, 1 - core)
    z_peers = [at(x, (z + d) % nz, core) for d in range(1, nz)]
    x_peers = [at((x + d) % nx, z, core) for d in range(1, nx)]
    y_peers = [(me, (head + d) % nh) for d in range(1, nh)]

    loads = {}
    for i, (name, src, dst) in enumerate((
        ("ld", ld_hbm, ld), ("k", k_hbm, k), ("v", v_hbm, v), ("q", q_hbm, q),
        ("gate", gate_hbm, gate), ("gout", gout_hbm, gout), ("gain", gain_hbm, gain),
    )):
        loads[name] = pltpu.make_async_copy(src, dst, local_sem.at[i])
        loads[name].start()
    barrier = pltpu.get_barrier_semaphore()
    peers = [partner] + z_peers + x_peers + y_peers
    for peer in peers:
        pl.semaphore_signal(barrier, inc=1, device_id=peer, device_id_type=MESH)

    started = []
    count = [0]

    def send(src, dst, device):
        copy = pltpu.make_async_remote_copy(
            src_ref=src, dst_ref=dst, send_sem=send_sem.at[count[0]],
            recv_sem=recv_sem.at[count[0]], device_id=device, device_id_type=MESH,
        )
        count[0] += 1
        copy.start()
        started.append(copy)
        return copy

    def arrived(copies):
        for copy in copies:
            copy.wait_recv()

    def lanes(h):
        return slice(h * DH, (h + 1) * DH)

    def stage_pair(own, par):
        return [send(own.at[1 - core], par, partner)]

    def first(reverse):
        return (core == 1) if reverse else (core == 0)

    def totals():
        tile_own = f_own[core, HALF:, :]
        tile_par = f_par[HALF:, :]
        return tile_own, tile_par

    def stage_chip(own, par, chip, zin, reverse):
        tile_own, tile_par = totals()
        one = jnp.ones_like(tile_own)
        w_own = jnp.where(first(reverse), jnp.exp(tile_par), one)
        w_par = jnp.where(first(reverse), one, jnp.exp(tile_own))
        both = jnp.exp(tile_own + tile_par)
        for zz in range(nz):
            at_row = zz * rows
            t = 4 * (at_row // DH)
            chip[zz, :rows, :] = (
                w_own[t : t + 1] * own[core, at_row : at_row + rows, :]
                + w_par[t : t + 1] * par[at_row : at_row + rows, :]
            )
            if not reverse:
                chip[zz, rows:, :] = jnp.broadcast_to(both[t : t + 1], (8, DH))
        zin[z] = chip[z]
        return [
            send(chip.at[(z + d) % nz], zin.at[z], z_peers[d - 1]) for d in range(1, nz)
        ]

    def order(n, reverse):
        return list(reversed(range(n))) if reverse else list(range(n))

    def stage_row(zin, xout, xin, state, reverse):
        total = jnp.zeros((rows, DH), F32)
        decay = jnp.ones((1, DH), F32)
        for zz in order(nz, reverse):
            state[zz, :rows, :] = total
            state[zz, rows:, :] = jnp.broadcast_to(decay, (8, DH))
            step = f_zin[zz, rows : rows + 1, :]
            total = step * total + zin[zz, :rows, :]
            decay = step * decay
        xout[:rows, :] = total
        xin[x, :rows, :] = total
        if not reverse:
            xout[rows:, :] = jnp.broadcast_to(decay, (8, DH))
            xin[x, rows:, :] = jnp.broadcast_to(decay, (8, DH))
        return [send(xout, xin.at[x], peer) for peer in x_peers]

    def stage_carry(xin, chip, back, state, reverse):
        carry = jnp.zeros((rows, DH), F32)
        for xx in order(nx, reverse):
            ahead = (xx > x) if reverse else (xx < x)
            step = f_xin[xx, rows : rows + 1, :]
            carry = jnp.where(ahead, step * carry + xin[xx, :rows, :], carry)
        for zz in range(nz):
            state[zz, :rows, :] = state[zz, :rows, :] + state[zz, rows : rows + 1, :] * carry
        back[z] = state[z, :rows, :]
        return [
            send(state.at[(z + d) % nz, pl.ds(0, rows)], back.at[z], z_peers[d - 1])
            for d in range(1, nz)
        ]

    def stage_split(own, par, back, ent, pair, reverse):
        tile_own, tile_par = totals()
        one, zero = jnp.ones_like(tile_own), jnp.zeros_like(tile_own)
        lead = first(reverse)
        w_own = jnp.where(lead, one, jnp.exp(tile_par))
        s_own = jnp.where(lead, zero, one)
        w_par = jnp.where(lead, jnp.exp(tile_own), one)
        s_par = jnp.where(lead, one, zero)
        for zz in range(nz):
            at_row = zz * rows
            t = 4 * (at_row // DH)
            here = slice(at_row, at_row + rows)
            entering = back[zz]
            pair[here, :] = (
                w_par[t : t + 1] * entering + s_par[t : t + 1] * own[core, here, :]
            )
        copies = [send(pair, ent.at[core], partner)]
        for zz in range(nz):
            at_row = zz * rows
            t = 4 * (at_row // DH)
            here = slice(at_row, at_row + rows)
            ent[core, here, :] = (
                w_own[t : t + 1] * back[zz] + s_own[t : t + 1] * par[here, :]
            )
        return copies

    loads["ld"].wait()
    cumul = lane_cumsum(jnp.concatenate([ld[...], ld[...]], axis=0))
    total = cumul[:, BLOCK - 1 :]
    a_row[...] = cumul
    ea_row[...] = jnp.exp(cumul)
    tail_row[...] = jnp.exp(total - cumul)
    for h in range(HEADS):
        f_own[h // 2, HALF + 4 * (h % 2) : HALF + 4 * (h % 2) + 4, :] = jnp.broadcast_to(
            total[h : h + 1], (4, DH)
        )

    loads["k"].wait()
    loads["v"].wait()
    for h in range(HEADS):
        weighted = (k[:, lanes(h)].T.astype(F32) * tail_row[h : h + 1, :]).astype(BF16)
        f_own[h // 2, (h % 2) * DH : (h % 2 + 1) * DH, :] = nn(weighted, v[:, lanes(h)])
    pl.semaphore_wait(barrier, len(peers))
    copies = stage_pair(f_own, f_par)

    def prepare(h):
        ea = columns(ea_row[h : h + 1, :])
        tail = columns(tail_row[h : h + 1, :])
        ea_col[h] = ea
        q_here = q[:, lanes(h)]
        wq[h] = (q_here.astype(F32) * ea).astype(BF16)
        wk[h] = (k[:, lanes(h)].astype(F32) * tail).astype(BF16)
        wv[h] = (v[:, lanes(h)].astype(F32) * tail).astype(BF16)
        qt[h] = q_here.T
        wqt[h] = (qt[h].astype(F32) * ea_row[h : h + 1, :]).astype(BF16)

    def intra(h):
        a_here = a_row[h : h + 1, :]
        a_col = columns(a_here)
        for t in range(0, BLOCK, TILE):
            seen = t + TILE
            here = slice(t, seen)
            scores = nt(q[here, lanes(h)], k[:seen, lanes(h)])
            col = jnp.concatenate([a_col[here]] * (seen // DH), axis=1)
            diff = col - a_here[:, :seen]
            keep = lax.broadcasted_iota(jnp.int32, diff.shape, 0) + t >= (
                lax.broadcasted_iota(jnp.int32, diff.shape, 1)
            )
            decay = jnp.where(keep, jnp.exp(jnp.where(keep, diff, 0.0)), 0.0)
            mask[h, here, :seen] = decay
            weights = (scores * decay).astype(BF16)
            fw[h, here, :seen] = weights
            att[here, lanes(h)] = nn(weights, v[:seen, lanes(h)])

    def gates(h):
        sig = jax.nn.sigmoid(gate[:, lanes(h)].astype(F32))
        normed = gout[:, lanes(h)].astype(F32) * sig * gain[:, lanes(h)]
        gn[:, lanes(h)] = normed
        gg[:, lanes(h)] = normed * (1.0 - sig)

    loads["q"].wait()
    prepare(0)
    intra(0)
    arrived(copies)
    copies = stage_chip(f_own, f_par, f_chip, f_zin, False)
    prepare(1)
    intra(1)
    prepare(2)
    intra(2)
    arrived(copies)
    copies = stage_row(f_zin, f_xout, f_xin, f_state, False)
    prepare(3)
    intra(3)
    arrived(copies)
    copies = stage_carry(f_xin, f_chip, f_back, f_state, False)
    for name in ("gate", "gout", "gain"):
        loads[name].wait()
    for h in range(HEADS):
        gates(h)
    arrived(copies)
    copies = stage_split(f_own, f_par, f_back, f_ent, f_pair, False)
    arrived(copies)

    def state_b(ent, h):
        return ent[h // 2, (h % 2) * DH : (h % 2 + 1) * DH, :].astype(BF16)

    squares = jnp.zeros((BLOCK, DH), F32)
    inner = jnp.zeros((BLOCK, DH), F32)
    for h in range(HEADS):
        full = att[:, lanes(h)] + nn(wq[h], state_b(f_ent, h))
        att[:, lanes(h)] = full
        squares = squares + full * full
        inner = inner + full * gn[:, lanes(h)]

    ones = jnp.ones((8, DH), BF16)

    def row_sums(value):
        high = value.astype(BF16)
        low = (value - high.astype(F32)).astype(BF16)
        return nt(ones, high) + nt(ones, low)

    sums = [row_sums(squares), row_sums(inner)]
    parts = BLOCK // DH
    y_out[...] = jnp.concatenate(
        [s[0:1, i * DH : (i + 1) * DH] for s in sums for i in range(parts)], axis=0
    )
    y_in[head] = y_out[...]
    copies = [send(y_out, y_in.at[head], peer) for peer in y_peers]
    arrived(copies)
    summed = y_in[0]
    for i in range(1, nh):
        summed = summed + y_in[i]
    features = HEADS * DH * nh
    rms = lax.rsqrt(summed[:parts] / features + 1e-05)
    coef = rms * rms * rms * summed[parts:] / features
    rms_col = jnp.concatenate([columns(rms[i : i + 1]) for i in range(parts)], axis=0)
    coef_col = jnp.concatenate([columns(coef[i : i + 1]) for i in range(parts)], axis=0)
    for h in range(HEADS):
        grad = (rms_col * gn[:, lanes(h)] - att[:, lanes(h)] * coef_col).astype(BF16)
        gb[:, lanes(h)] = grad
        r_own[h // 2, (h % 2) * DH : (h % 2 + 1) * DH, :] = nn(wqt[h], grad)
    copies = stage_pair(r_own, r_par)

    stores = []

    def store(src, dst):
        copy = pltpu.make_async_copy(src, dst, local_sem.at[7 + len(stores)])
        copy.start()
        stores.append(copy)

    def back(h):
        grad = gb[:, lanes(h)]
        entering = state_b(f_ent, h)
        upper = []
        for t in range(0, BLOCK, TILE):
            seen = t + TILE
            here = slice(t, seen)
            weights = (nt(grad[here], v[:seen, lanes(h)]) * mask[h, here, :seen]).astype(BF16)
            upper.append(weights)
            dq[here, lanes(h)] = (
                nn(weights, k[:seen, lanes(h)]) + ea_col[h, here, :] * nt(grad[here], entering)
            ).astype(BF16)
        gt = grad.T
        for s in range(0, BLOCK, TILE):
            here = slice(s, s + TILE)
            key = value = None
            for t in range(s, BLOCK, TILE):
                there = slice(t, t + TILE)
                one_key = nn(qt[h, :, there], upper[t // TILE][:, here])
                one_value = nn(gt[:, there], fw[h, there, here])
                key = one_key if key is None else key + one_key
                value = one_value if value is None else value + one_value
            dki[here, lanes(h)] = key.T
            dvi[here, lanes(h)] = value.T

    back(0)
    arrived(copies)
    copies = stage_chip(r_own, r_par, r_chip, r_zin, True)
    back(1)
    back(2)
    arrived(copies)
    copies = stage_row(r_zin, r_xout, r_xin, r_state, True)
    back(3)
    arrived(copies)
    copies = stage_carry(r_xin, r_chip, r_back, r_state, True)
    store(dq, dq_hbm)
    for h in range(HEADS):
        dg[:, lanes(h)] = (gg[:, lanes(h)] * att[:, lanes(h)] * rms_col).astype(BF16)
    store(dg, dg_hbm)
    arrived(copies)
    copies = stage_split(r_own, r_par, r_back, r_ent, r_pair, True)
    arrived(copies)
    for h in range(HEADS):
        leaving = state_b(r_ent, h)
        dk[:, lanes(h)] = (dki[:, lanes(h)] + nt(wv[h], leaving)).astype(BF16)
        dv[:, lanes(h)] = (dvi[:, lanes(h)] + nn(wk[h], leaving)).astype(BF16)
    store(dk, dk_hbm)
    store(dv, dv_hbm)
    for copy in started:
        copy.wait_send()
    for copy in stores:
        copy.wait()


def build(nx, nz, nh):
    rows = HALF // nz
    wide = (BLOCK, HEADS * DH)
    per_head = (HEADS, BLOCK, DH)

    def vmem(shape, dtype=F32):
        return pltpu.VMEM(shape, dtype)

    def scan_scratch(extra):
        return [
            vmem((2, HALF + extra, DH)),
            vmem((HALF + extra, DH)),
            vmem((nz, rows + extra, DH)),
            vmem((nz, rows + extra, DH)),
            vmem((rows + extra, DH)),
            vmem((nx, rows + extra, DH)),
            vmem((nz, rows, DH)),
            vmem((2, HALF, DH)),
            vmem((HALF, DH)),
            vmem((nz, rows + 8, DH)),
        ]

    n_copies = 2 * (2 + 2 * (nz - 1) + nx - 1) + nh - 1
    scratch = (
        [vmem(wide, BF16)] * 5
        + [vmem((HEADS, BLOCK)), vmem((1, HEADS * DH))]
        + [vmem(wide, BF16)] * 4
        + [vmem((8, BLOCK))] * 3
        + [vmem(per_head)] * 2
        + [vmem((HEADS, DH, BLOCK), BF16)] * 2
        + [vmem(per_head, BF16)] * 3
        + [vmem((HEADS, BLOCK, BLOCK)), vmem((HEADS, BLOCK, BLOCK), BF16)]
        + [vmem(wide)] * 3
        + [vmem(wide, BF16)]
        + [vmem(wide)] * 2
        + scan_scratch(8)
        + scan_scratch(0)
        + [vmem((8, DH)), vmem((nh, 8, DH))]
        + [
            pltpu.SemaphoreType.DMA((11,)),
            pltpu.SemaphoreType.DMA((n_copies,)),
            pltpu.SemaphoreType.DMA((n_copies,)),
        ]
    )

    def local(q, k, v, gate, gout, log_decay, gain):
        any_space = pl.BlockSpec(memory_space=pl.ANY)
        return tuple(
            pl.pallas_call(
                functools.partial(kernel, nx, nz, nh),
                out_shape=[jax.ShapeDtypeStruct(wide, BF16)] * 4,
                in_specs=[any_space] * 7,
                out_specs=[any_space] * 4,
                scratch_shapes=scratch,
                compiler_params=pltpu.CompilerParams(
                    collective_id=0, has_side_effects=True, vmem_limit_bytes=56 * 2**20
                ),
            )(q, k, v, gate, gout, log_decay.T, gain.reshape(1, HEADS * DH))
        )

    return local


def solution(mesh):
    nx, nz = NX, NZ
    if mesh.shape["ctx"] != 2 * nx * nz:
        nx = nz = 2
    part = P("ctx", "head")
    return jax.shard_map(
        build(nx, nz, mesh.shape["head"]),
        mesh=mesh,
        in_specs=(part,) * 6 + (P("head"),),
        out_specs=(part,) * 4,
        check_vma=False,
    )
```

time: 398 us -> 65.7 us (0.17)
  waiting for transfers between devices: 220 us -> 0 us
  other arithmetic: 72.7 us -> 0 us
  Pallas kernels: 0 us -> 59.6 us
  blocking collectives: 59.6 us -> 0 us
  matrix products: 15.6 us -> 0 us
  between operations: 14.4 us -> 0.65 us
  local copies, waits for them, and re-layouts: 10.8 us -> 5.18 us
    all_gather x2 -> x0, waiting for transfers between devices: 220 us -> none  [carried_in(): gathered = jax.tree.map(lambda a: lax.all_gather(a, axis), part)]
    add x63 -> x0, other arithmetic: 66.8 us -> none  [the longest x62 65.8 us: join_reverse(): later_part[1] + later_part[0][:, None, None] * earlier_part[1]]
    pallas_call x0 -> x1, Pallas kernels: none -> 59.6 us  [local(): pl.pallas_call(functools.partial(kernel, nx, nz, nh), out_shape=[jax.Shap...]
    all_gather x1 -> x0, blocking collectives: 46.4 us -> none  [carried_in(): gathered = jax.tree.map(lambda a: lax.all_gather(a, axis), part)]
    dot_general x12 -> x0, matrix products: 15.6 us -> none  [the longest x1 2.75 us: local(): jnp.einsum('nthv,nhkv->nthk', grad_blk, entering_b, preferred_element_typ...]
    psum x1 -> x0, blocking collectives: 13.2 us -> none  [local(): squares, inner_sum = lax.psum((row_squares, row_inner), 'head')]
  transfers between devices with their start and end apart: 2 -> 0, of which waited for: 2 -> 0; matrix products, arithmetic and copies ran while one was open for 3% -> 0% of each run, Pallas kernels for 0% -> 0%
where the time goes in v1:
time: 65.7 us; the launch traced here: 65.4 us
  Pallas kernels  59.6 us (91%)
  local copies, waits for them, and re-layouts  5.18 us (8%)
    pallas_call x1, Pallas kernels, local(): pl.pallas_call(functools.partial(kernel, nx, nz, nh), out_shape=[jax.Shap...  59.6 us
    unnamed x10, local copies, waits for them, and re-layouts  5.18 us

profile of v1, /device:TPU:1, one launch (start us, length us, event | category | flops | bytes accessed | tf_op | source)
XLA Modules:
  0.0 65.4 jit_solution(7438295479359711062)
XLA Ops:
  0.6 59.6 %shard_map.102 = (bf16[512,512]{1,0:T(8,128)(2,1)}, bf16[512,512]{1,0:T(8,128)(2,1)}, bf16[512,512]{1,0:T(8,128)(2,1)}, bf16[512,512]{1,0:T(8,128)(2,1)}) custom-call(bf16[512,512]{1,0:T(8,128)(2,1)} %q_hbm.1, bf16[512,512]{1,0:T(8,128)(2,1)} %k_hbm.1, bf16[512,512]{1,0:T(8,128)(2,1)} %v_hbm.1, bf16[512,512]{1,0:T(8,128)(2,1)} %gate_hbm.1, ...), custom_call_target="tpu_custom_call" | custom-call | tf_op jit(solution)/shard_map/pallas_call | solution.py:416
  60.2 0.0 copy-start.2
  60.2 1.9 %copy.15 = bf16[512,512]{1,0:T(8,128)(2,1)} copy(bf16[512,512]{1,0:T(8,128)(2,1)} %get-tuple-element.8) | data formatting | bytes 1048576
  62.2 0.0 copy-done.2
  62.2 0.0 copy-start.1
  62.2 0.8 %copy.16 = bf16[512,512]{1,0:T(8,128)(2,1)} copy(bf16[512,512]{1,0:T(8,128)(2,1)S(1)} %copy-done.2) | data formatting | bytes 1048576
  63.0 0.4 copy-done.1
  63.4 0.0 copy-start
  63.4 0.8 %copy.17 = bf16[512,512]{1,0:T(8,128)(2,1)} copy(bf16[512,512]{1,0:T(8,128)(2,1)S(1)} %copy-done.1) | data formatting | bytes 1048576
  64.2 0.4 copy-done
  64.6 0.8 %copy.18 = bf16[512,512]{1,0:T(8,128)(2,1)} copy(bf16[512,512]{1,0:T(8,128)(2,1)S(1)} %copy-done) | data formatting | bytes 1048576
Async XLA Ops:
  60.2 1.9 %copy-start.2 = (bf16[512,512]{1,0:T(8,128)(2,1)S(1)}, bf16[512,512]{1,0:T(8,128)(2,1)}, u32[]{:S(2)}) copy-start(bf16[512,512]{1,0:T(8,128)(2,1)} %get-tuple-element.9) | copy-start | bytes 1572868
  62.2 1.2 %copy-start.1 = (bf16[512,512]{1,0:T(8,128)(2,1)S(1)}, bf16[512,512]{1,0:T(8,128)(2,1)}, u32[]{:S(2)}) copy-start(bf16[512,512]{1,0:T(8,128)(2,1)} %get-tuple-element.10) | copy-start | bytes 1572868
  63.4 1.2 %copy-start = (bf16[512,512]{1,0:T(8,128)(2,1)S(1)}, bf16[512,512]{1,0:T(8,128)(2,1)}, u32[]{:S(2)}) copy-start(bf16[512,512]{1,0:T(8,128)(2,1)} %get-tuple-element.11) | copy-start | bytes 1572868

commit v2 on v1

v2 whole, which is shorter than its diff:
```python
import functools

import jax
import jax.numpy as jnp
from jax import lax
from jax.experimental import pallas as pl
from jax.experimental.pallas import tpu as pltpu
from jax.sharding import PartitionSpec as P

BLOCK = 512
DH = 128
HEADS = 4
HALF = HEADS // 2
TILE = 256
NX = 4
NZ = 8
F32 = jnp.float32
BF16 = jnp.bfloat16
MESH = pl.DeviceIdType.MESH


def nn(a, b):
    return jnp.dot(a, b, preferred_element_type=F32)


def nt(a, b):
    return lax.dot_general(a, b, (((1,), (1,)), ((), ())), preferred_element_type=F32)


def lane_cumsum(x):
    place = lax.broadcasted_iota(jnp.int32, x.shape, 1)
    step = 1
    while step < x.shape[1]:
        x = x + jnp.where(place >= step, pltpu.roll(x, step, 1), 0.0)
        step *= 2
    return x


def turned(rows):
    pad = jnp.zeros((DH - rows.shape[0], rows.shape[1]), F32)
    return jnp.concatenate([rows, pad], axis=0).T


def kept(shape, dtype):
    return pltpu.VMEM(shape, dtype)


def placed(values, space):
    return [pltpu.with_memory_space_constraint(value, space) for value in values]


def lanes(h):
    return slice(h * DH, (h + 1) * DH)


def kernel(
    nx, nz, nh,
    q_hbm, k_hbm, v_hbm, gate_hbm, gout_hbm, ld_hbm, gain_hbm,
    dq, dg, dki, dvi, wk, wv, r_ent,
    q, k, v, gate, gout, ld, gain,
    row_form, col_form, ea_col,
    qt, wqt, wq, mask, fw, att, gn, gg, gb,
    g_own, g_par, g_all, decay,
    f_own, f_par, f_chip, f_zin, f_back, f_ent, f_pair, f_pre,
    r_own, r_par, r_chip, r_zin, r_back, r_pair, r_pre,
    y_out, y_in,
    local_sem, send_sem, recv_sem,
):
    me, head = lax.axis_index("ctx"), lax.axis_index("head")
    core, chip_at = me % 2, me // 2
    z, x = chip_at % nz, chip_at // nz
    chips = nx * nz
    rows = HALF * DH // chips
    per_head = chips // HALF

    def at(xx, zz, cc):
        return ((xx * nz + zz) * 2 + cc, head)

    partner = at(x, z, 1 - core)
    far_first = sorted(range(nz), key=lambda d: -min(d, nz - d))
    steps = [(dx, dz) for dz in far_first for dx in range(nx) if (dx, dz) != (0, 0)]
    others = [((x + dx) % nx, (z + dz) % nz) for dx, dz in steps]
    z_peers = [at(x, (z + d) % nz, core) for d in range(1, nz)]
    x_peers = [at((x + d) % nx, z, core) for d in range(1, nx)]
    chip_peers = [at(xx, zz, core) for xx, zz in others]
    y_peers = [(me, (head + d) % nh) for d in range(1, nh)]

    loads = {}
    for i, (name, src, dst) in enumerate((
        ("ld", ld_hbm, ld), ("k", k_hbm, k), ("v", v_hbm, v), ("q", q_hbm, q),
        ("gate", gate_hbm, gate), ("gout", gout_hbm, gout), ("gain", gain_hbm, gain),
    )):
        loads[name] = pltpu.make_async_copy(src, dst, local_sem.at[i])
        loads[name].start()
    barrier = pltpu.get_barrier_semaphore()
    peers = [partner] + chip_peers + y_peers
    for peer in peers:
        pl.semaphore_signal(barrier, inc=1, device_id=peer, device_id_type=MESH)

    sent = []
    stage = [0]

    def send(copies, span):
        mine, stage[0] = stage[0], stage[0] + 1
        for src, dst, device in copies:
            pltpu.make_async_remote_copy(
                src_ref=src, dst_ref=dst, send_sem=send_sem.at[mine],
                recv_sem=recv_sem.at[mine], device_id=device, device_id_type=MESH,
            ).start()
        sent.append((mine, span))
        return mine, span

    def arrived(handle):
        mine, span = handle
        pltpu.make_async_copy(span, span, recv_sem.at[mine]).wait()

    def first(reverse):
        return (core == 1) if reverse else (core == 0)

    def decay_row(ref, i):
        return jnp.exp(ref[pl.ds(HALF * core + i, 1), :])

    def part(i):
        return slice(i * per_head, (i + 1) * per_head)

    def stage_pair(own, par):
        return send([(own.at[1 - core], par, partner)], par)

    def stage_chip(own, par, chip, zin, reverse):
        one = jnp.ones((1, DH), F32)
        for i in range(HALF):
            w_own = jnp.where(first(reverse), decay_row(g_par, i), one)
            w_par = jnp.where(first(reverse), one, decay_row(g_own, i))
            chip[part(i)] = w_own * own[core, part(i)] + w_par * par[part(i)]
        handle = send(
            [
                (chip.at[xx * nz + zz], zin.at[chip_at], device)
                for (xx, zz), device in zip(others, chip_peers)
            ],
            zin.at[pl.ds(0, chips - 1)],
        )
        zin[chip_at] = chip[chip_at]
        return handle

    def stage_fold(zin, pre, back, reverse):
        total = jnp.zeros((rows, DH), F32)
        for j in reversed(range(chips)) if reverse else range(chips):
            pre[j] = total
            total = decay[j, 0:1, :] * total + zin[j]
        handle = send(
            [
                (pre.at[xx * nz + zz], back.at[chip_at], device)
                for (xx, zz), device in zip(others, chip_peers)
            ],
            back.at[pl.ds(0, chips - 1)],
        )
        back[chip_at] = pre[chip_at]
        return handle

    def stage_split(own, par, back, ent, pair, reverse):
        one, zero = jnp.ones((1, DH), F32), jnp.zeros((1, DH), F32)
        lead = first(reverse)
        for i in range(HALF):
            w_par = jnp.where(lead, decay_row(g_own, i), one)
            s_par = jnp.where(lead, one, zero)
            pair[part(i)] = w_par * back[part(i)] + s_par * own[core, part(i)]
        handle = send([(pair, ent.at[core], partner)], pair)
        for i in range(HALF):
            w_own = jnp.where(lead, one, decay_row(g_par, i))
            s_own = jnp.where(lead, zero, one)
            ent[core, part(i)] = w_own * back[part(i)] + s_own * par[part(i)]
        return handle

    def state_b(ent, h):
        return ent[h // HALF, part(h % HALF)].reshape(DH, DH).astype(BF16)

    loads["ld"].wait()
    cumul = lane_cumsum(jnp.concatenate([ld[...], ld[...]], axis=0))
    total = cumul[:, BLOCK - 1 :]
    g_own[...] = jnp.broadcast_to(total, (8, DH))
    ea, tail = jnp.exp(cumul), jnp.exp(total - cumul)
    row_form[0], row_form[1], row_form[2] = cumul, ea, tail
    pl.semaphore_wait(barrier, len(peers))
    g_copies = send([(g_own, g_par, partner)], g_par)

    loads["k"].wait()
    loads["v"].wait()
    for h in range(HEADS):
        weighted = (k[:, lanes(h)].T.astype(F32) * tail[h : h + 1, :]).astype(BF16)
        f_own[h // HALF, part(h % HALF)] = nn(weighted, v[:, lanes(h)]).reshape(
            per_head, rows, DH
        )
    copies = stage_pair(f_own, f_par)
    arrived(g_copies)
    g_all[chip_at] = g_own[...] + g_par[...]
    g_copies = send(
        [(g_all.at[chip_at], g_all.at[chip_at], peer) for peer in z_peers],
        g_all.at[pl.ds(0, nz - 1)],
    )

    col_form[...] = turned(jnp.concatenate([cumul, ea, tail], axis=0))

    def column(kind, h):
        j = 8 * kind + h
        return jnp.broadcast_to(col_form[:, j : j + 1], (BLOCK, DH))

    def prepare(h):
        ea_here = column(1, h)
        tail_here = column(2, h)
        ea_col[h] = ea_here
        q_here = q[:, lanes(h)]
        wq[h] = (q_here.astype(F32) * ea_here).astype(BF16)
        wk[:, lanes(h)] = (k[:, lanes(h)].astype(F32) * tail_here).astype(BF16)
        wv[:, lanes(h)] = (v[:, lanes(h)].astype(F32) * tail_here).astype(BF16)
        turned_q = q_here.T
        qt[h] = turned_q
        wqt[h] = (turned_q.astype(F32) * row_form[1, h : h + 1, :]).astype(BF16)

    def intra(h):
        a_here = row_form[0, h : h + 1, :]
        a_col = column(0, h)
        for t in range(0, BLOCK, TILE):
            seen = t + TILE
            here = slice(t, seen)
            scores = nt(q[here, lanes(h)], k[:seen, lanes(h)])
            col = jnp.concatenate([a_col[here]] * (seen // DH), axis=1)
            diff = col - a_here[:, :seen]
            keep = lax.broadcasted_iota(jnp.int32, diff.shape, 0) + t >= (
                lax.broadcasted_iota(jnp.int32, diff.shape, 1)
            )
            weight = jnp.where(keep, jnp.exp(jnp.where(keep, diff, 0.0)), 0.0)
            mask[h, here, :seen] = weight
            weights = (scores * weight).astype(BF16)
            fw[h, here, :seen] = weights
            att[here, lanes(h)] = nn(weights, v[:seen, lanes(h)])

    def gates(h):
        sig = jax.nn.sigmoid(gate[:, lanes(h)].astype(F32))
        normed = gout[:, lanes(h)].astype(F32) * sig * gain[:, lanes(h)]
        gn[:, lanes(h)] = normed
        gg[:, lanes(h)] = normed * (1.0 - sig)

    loads["q"].wait()
    prepare(0)
    arrived(g_copies)
    row_at = pl.ds(x * nz, nz)
    g_copies = send(
        [(g_all.at[row_at], g_all.at[row_at], peer) for peer in x_peers],
        g_all.at[pl.ds(0, nz * (nx - 1))],
    )
    arrived(copies)
    copies = stage_chip(f_own, f_par, f_chip, f_zin, False)
    intra(0)
    prepare(1)
    intra(1)
    prepare(2)
    intra(2)
    arrived(g_copies)
    mine = HALF * core + chip_at * rows // DH
    for j in range(chips):
        decay[j] = jnp.broadcast_to(jnp.exp(g_all[j, pl.ds(mine, 1), :]), (8, DH))
    arrived(copies)
    copies = stage_fold(f_zin, f_pre, f_back, False)
    prepare(3)
    intra(3)
    for name in ("gate", "gout", "gain"):
        loads[name].wait()
    for h in range(HEADS):
        gates(h)
    arrived(copies)
    copies = stage_split(f_own, f_par, f_back, f_ent, f_pair, False)
    arrived(copies)

    squares = jnp.zeros((BLOCK, DH), F32)
    inner = jnp.zeros((BLOCK, DH), F32)
    for h in range(HEADS):
        full = att[:, lanes(h)] + nn(wq[h], state_b(f_ent, h))
        att[:, lanes(h)] = full
        squares = squares + full * full
        inner = inner + full * gn[:, lanes(h)]

    ones = jnp.ones((8, DH), BF16)

    def row_sums(value):
        high = value.astype(BF16)
        low = (value - high.astype(F32)).astype(BF16)
        return nt(ones, high) + nt(ones, low)

    sums = [row_sums(squares), row_sums(inner)]
    parts = BLOCK // DH
    y_out[...] = jnp.concatenate(
        [s[0:1, i * DH : (i + 1) * DH] for s in sums for i in range(parts)], axis=0
    )
    copies = send(
        [(y_out, y_in.at[head], peer) for peer in y_peers], y_in.at[pl.ds(0, nh - 1)]
    )
    y_in[head] = y_out[...]
    arrived(copies)
    summed = y_in[0]
    for i in range(1, nh):
        summed = summed + y_in[i]
    features = HEADS * DH * nh
    rms = lax.rsqrt(summed[:parts] / features + 1e-05)
    coef = rms * rms * rms * summed[parts:] / features
    scales = turned(jnp.concatenate([rms, coef], axis=0))

    def scale_column(first_lane):
        return jnp.concatenate(
            [
                jnp.broadcast_to(scales[:, i : i + 1], (DH, DH))
                for i in range(first_lane, first_lane + parts)
            ],
            axis=0,
        )

    rms_col, coef_col = scale_column(0), scale_column(parts)
    for h in range(HEADS):
        grad = (rms_col * gn[:, lanes(h)] - att[:, lanes(h)] * coef_col).astype(BF16)
        gb[:, lanes(h)] = grad
        r_own[h // HALF, part(h % HALF)] = nn(wqt[h], grad).reshape(per_head, rows, DH)
    copies = stage_pair(r_own, r_par)

    def back(h):
        grad = gb[:, lanes(h)]
        entering = state_b(f_ent, h)
        upper = []
        for t in range(0, BLOCK, TILE):
            seen = t + TILE
            here = slice(t, seen)
            weights = (nt(grad[here], v[:seen, lanes(h)]) * mask[h, here, :seen]).astype(BF16)
            upper.append(weights)
            dq[here, lanes(h)] = (
                nn(weights, k[:seen, lanes(h)]) + ea_col[h, here, :] * nt(grad[here], entering)
            ).astype(BF16)
        gt = grad.T
        for s in range(0, BLOCK, TILE):
            here = slice(s, s + TILE)
            key = value = None
            for t in range(s, BLOCK, TILE):
                there = slice(t, t + TILE)
                one_key = nn(qt[h, :, there], upper[t // TILE][:, here])
                one_value = nn(gt[:, there], fw[h, there, here])
                key = one_key if key is None else key + one_key
                value = one_value if value is None else value + one_value
            dki[here, lanes(h)] = key.T
            dvi[here, lanes(h)] = value.T

    for h in range(HEADS):
        dg[:, lanes(h)] = (gg[:, lanes(h)] * att[:, lanes(h)] * rms_col).astype(BF16)
    arrived(copies)
    copies = stage_chip(r_own, r_par, r_chip, r_zin, True)
    back(0)
    back(1)
    arrived(copies)
    copies = stage_fold(r_zin, r_pre, r_back, True)
    back(2)
    back(3)
    arrived(copies)
    copies = stage_split(r_own, r_par, r_back, r_ent, r_pair, True)
    arrived(copies)
    for mine, span in sent:
        pltpu.make_async_copy(span, span, send_sem.at[mine]).wait()


def finish(
    dq_in, dg_in, dki, dvi, wk, wv, ent, dq_hbm, dk_hbm, dv_hbm, dg_hbm, dk, dv, sem
):
    copies = [
        pltpu.make_async_copy(dq_in, dq_hbm, sem.at[0]),
        pltpu.make_async_copy(dg_in, dg_hbm, sem.at[1]),
    ]
    for copy in copies:
        copy.start()
    for h in range(HEADS):
        leaving = ent[h].astype(BF16)
        dk[:, lanes(h)] = (dki[:, lanes(h)] + nt(wv[:, lanes(h)], leaving)).astype(BF16)
        dv[:, lanes(h)] = (dvi[:, lanes(h)] + nn(wk[:, lanes(h)], leaving)).astype(BF16)
        for i, (src, dst) in enumerate(((dk, dk_hbm), (dv, dv_hbm))):
            copy = pltpu.make_async_copy(
                src.at[:, lanes(h)], dst.at[:, lanes(h)], sem.at[2 + 2 * h + i]
            )
            copy.start()
            copies.append(copy)
    for copy in copies:
        copy.wait()


def build(nx, nz, nh):
    chips = nx * nz
    rows = HALF * DH // chips
    wide = (BLOCK, HEADS * DH)
    per_head = (HEADS, BLOCK, DH)

    def vmem(shape, dtype=F32):
        return pltpu.VMEM(shape, dtype)

    shards, halves = vmem((chips, rows, DH)), vmem((HALF, chips, rows, DH))
    scratch = (
        [vmem(wide, BF16)] * 5
        + [vmem((HEADS, BLOCK)), vmem((1, HEADS * DH))]
        + [vmem((3, 8, BLOCK)), vmem((BLOCK, DH)), vmem(per_head)]
        + [vmem((HEADS, DH, BLOCK), BF16)] * 2
        + [vmem(per_head, BF16)]
        + [vmem((HEADS, BLOCK, BLOCK)), vmem((HEADS, BLOCK, BLOCK), BF16)]
        + [vmem(wide)] * 3
        + [vmem(wide, BF16)]
        + [vmem((8, DH))] * 2
        + [vmem((chips, 8, DH))] * 2
        + [halves, shards, shards, shards, shards, halves, shards, shards]
        + [halves, shards, shards, shards, shards, shards, shards]
        + [vmem((8, DH)), vmem((nh, 8, DH))]
        + [pltpu.SemaphoreType.DMA((7,))]
        + [pltpu.SemaphoreType.DMA((12,))] * 2
    )
    any_space = pl.BlockSpec(memory_space=pl.ANY)
    in_vmem = pl.BlockSpec(memory_space=pltpu.VMEM)

    def local(q, k, v, gate, gout, log_decay, gain):
        made = pl.pallas_call(
            functools.partial(kernel, nx, nz, nh),
            out_shape=[kept(wide, BF16)] * 2
            + [kept(wide, F32)] * 2
            + [kept(wide, BF16)] * 2
            + [kept((HALF, chips, rows, DH), F32)],
            in_specs=[any_space] * 7,
            out_specs=[in_vmem] * 7,
            scratch_shapes=scratch,
            compiler_params=pltpu.CompilerParams(
                collective_id=0, has_side_effects=True, vmem_limit_bytes=36 * 2**20
            ),
        )(*placed(
            (q, k, v, gate, gout, log_decay.T, gain.reshape(1, HEADS * DH)), pltpu.HBM
        ))
        made = list(made)
        made[-1] = made[-1].reshape(HEADS, DH, DH)
        return tuple(
            pl.pallas_call(
                finish,
                out_shape=[jax.ShapeDtypeStruct(wide, BF16)] * 4,
                in_specs=[in_vmem] * 7,
                out_specs=[any_space] * 4,
                scratch_shapes=[vmem(wide, BF16)] * 2 + [pltpu.SemaphoreType.DMA((10,))],
                compiler_params=pltpu.CompilerParams(vmem_limit_bytes=8 * 2**20),
            )(*placed(made, pltpu.VMEM))
        )

    return local


def solution(mesh):
    nx, nz = NX, NZ
    if mesh.shape["ctx"] != 2 * nx * nz:
        nx = nz = 2
    part = P("ctx", "head")
    return jax.shard_map(
        build(nx, nz, mesh.shape["head"]),
        mesh=mesh,
        in_specs=(part,) * 6 + (P("head"),),
        out_specs=(part,) * 4,
        check_vma=False,
    )
```

time: 65.7 us -> 59 us (0.90)
  local copies, waits for them, and re-layouts: 5.18 us -> 0 us
  Pallas kernels: 59.6 us -> 58.2 us
    unnamed x10 -> x0, local copies, waits for them, and re-layouts: 5.18 us -> none
    pallas_call x1 -> x2, Pallas kernels: 59.6 us -> 58.2 us  [the longest x1 56.8 us: local(): pl.pallas_call(functools.partial(kernel, nx, nz, nh), out_shape=[kept(wid...]
where the time goes in v2:
time: 59 us; the launch traced here: 58.9 us
  Pallas kernels  58.2 us (99%)
  between operations  0.64 us (1%)
    pallas_call x1, Pallas kernels, local(): pl.pallas_call(functools.partial(kernel, nx, nz, nh), out_shape=[kept(wid...  56.8 us
    pallas_call x1, Pallas kernels, local(): pl.pallas_call(finish, out_shape=[jax.ShapeDtypeStruct(wide, BF16)] * 4,...  1.39 us

profile of v2, /device:TPU:1, one launch (start us, length us, event | category | flops | bytes accessed | tf_op | source)
XLA Modules:
  0.0 58.9 jit_solution(11300299380722190153)
XLA Ops:
  0.6 56.8 %shard_map.102 = (bf16[512,512]{1,0:T(8,128)(2,1)S(1)}, bf16[512,512]{1,0:T(8,128)(2,1)S(1)}, f32[512,512]{1,0:T(8,128)S(1)}, f32[512,512]{1,0:T(8,128)S(1)}, bf...) custom-call(bf16[512,512]{1,0:T(8,128)(2,1)} %q_hbm.1, ...), custom_call_target="tpu_custom_call" | custom-call | tf_op jit(solution)/shard_map/pallas_call | solution.py:419
  57.5 1.4 %shard_map.103 = (bf16[512,512]{1,0:T(8,128)(2,1)}, bf16[512,512]{1,0:T(8,128)(2,1)}, bf16[512,512]{1,0:T(8,128)(2,1)}, bf16[512,512]{1,0:T(8,128)(2,1)}) custom-call(bf16[512,512]{1,0:T(8,128)(2,1)S(1)} %get-tuple-element.11.dq_in, bf16[512,512]{1,0:T(8,128)(2,1)S(1)} %get-tuple-element.12.dg_in, f32[512,512]{1,0:T(8,128)S(1)} %get-tuple-element.13.dki, ...), custom_call_target="tpu_custom_call" | custom-call | tf_op jit(solution)/shard_map/pallas_call | solution.py:437

commit v3 on v2

--- a/solution.py
+++ b/solution.py
@@ -77,13 +77,20 @@
         return ((xx * nz + zz) * 2 + cc, head)
 
     partner = at(x, z, 1 - core)
-    far_first = sorted(range(nz), key=lambda d: -min(d, nz - d))
-    steps = [(dx, dz) for dz in far_first for dx in range(nx) if (dx, dz) != (0, 0)]
-    others = [((x + dx) % nx, (z + dz) % nz) for dx, dz in steps]
+    sign = 1 - 2 * core
+
+    def shifted(place, d, n):
+        return (place + n + sign * d) % n
+
+    def outward(n):
+        return sorted(range(n), key=lambda d: -min(d, n - d))
+
+    steps = [(dx, dz) for dx in outward(nx) for dz in outward(nz) if (dx, dz) != (0, 0)]
+    others = [(shifted(x, dx, nx), shifted(z, dz, nz)) for dx, dz in steps]
     z_peers = [at(x, (z + d) % nz, core) for d in range(1, nz)]
     x_peers = [at((x + d) % nx, z, core) for d in range(1, nx)]
     chip_peers = [at(xx, zz, core) for xx, zz in others]
-    y_peers = [(me, (head + d) % nh) for d in range(1, nh)]
+    y_peers = [(me, shifted(head, d, nh)) for d in outward(nh) if d]
 
     loads = {}
     for i, (name, src, dst) in enumerate((
@@ -98,15 +105,22 @@
         pl.semaphore_signal(barrier, inc=1, device_id=peer, device_id_type=MESH)
 
     sent = []
-    stage = [0]
+    used = [0]
+
+    def fresh(n=1):
+        used[0] += n
+        return used[0] - n
+
+    def start(src, dst, device, send_at, recv_at):
+        pltpu.make_async_remote_copy(
+            src_ref=src, dst_ref=dst, send_sem=send_sem.at[send_at],
+            recv_sem=recv_sem.at[recv_at], device_id=device, device_id_type=MESH,
+        ).start()
 
     def send(copies, span):
-        mine, stage[0] = stage[0], stage[0] + 1
+        mine = fresh()
         for src, dst, device in copies:
-            pltpu.make_async_remote_copy(
-                src_ref=src, dst_ref=dst, send_sem=send_sem.at[mine],
-                recv_sem=recv_sem.at[mine], device_id=device, device_id_type=MESH,
-            ).start()
+            start(src, dst, device, mine, mine)
         sent.append((mine, span))
         return mine, span
 
@@ -123,52 +137,71 @@
     def part(i):
         return slice(i * per_head, (i + 1) * per_head)
 
-    def stage_pair(own, par):
-        return send([(own.at[1 - core], par, partner)], par)
-
-    def stage_chip(own, par, chip, zin, reverse):
+    parity = z % 2
+    my_shard = parity * per_head + chip_at // 2
+    pairs = nz // 2
+
+    def stage_pair(own, par, i):
+        here = pl.ds(i * per_head, per_head)
+        return send([(own.at[1 - core, here], par.at[here], partner)], par.at[here])
+
+    def stage_chip(own, par, chip, zin, i, sems, reverse):
         one = jnp.ones((1, DH), F32)
-        for i in range(HALF):
-            w_own = jnp.where(first(reverse), decay_row(g_par, i), one)
-            w_par = jnp.where(first(reverse), one, decay_row(g_own, i))
-            chip[part(i)] = w_own * own[core, part(i)] + w_par * par[part(i)]
-        handle = send(
-            [
-                (chip.at[xx * nz + zz], zin.at[chip_at], device)
-                for (xx, zz), device in zip(others, chip_peers)
-            ],
-            zin.at[pl.ds(0, chips - 1)],
-        )
-        zin[chip_at] = chip[chip_at]
-        return handle
-
-    def stage_fold(zin, pre, back, reverse):
+        w_own = jnp.where(first(reverse), decay_row(g_par, i), one)
+        w_par = jnp.where(first(reverse), one, decay_row(g_own, i))
+        chip[part(i)] = w_own * own[core, part(i)] + w_par * par[part(i)]
+
+        def post(xx, zz):
+            shard = i * per_head + (xx * nz + zz) // 2
+            start(chip.at[shard], zin.at[chip_at], at(xx, zz, core), sems, sems)
+
+        for dx in outward(nx):
+            for p in outward(pairs):
+                if p or dx:
+                    post(shifted(x, dx, nx), 2 * shifted(z // 2, p, pairs) + i)
+
+        @pl.when(parity != i)
+        def _():
+            post(x, 2 * (z // 2) + i)
+
+        @pl.when(parity == i)
+        def _():
+            zin[chip_at] = chip[my_shard]
+
+    def stage_fold(zin, pre, back, sems, reverse):
+        all_others = zin.at[pl.ds(0, chips - 1)]
+        arrived((sems, all_others))
+        sent.append((sems, all_others))
         total = jnp.zeros((rows, DH), F32)
         for j in reversed(range(chips)) if reverse else range(chips):
             pre[j] = total
             total = decay[j, 0:1, :] * total + zin[j]
-        handle = send(
-            [
-                (pre.at[xx * nz + zz], back.at[chip_at], device)
-                for (xx, zz), device in zip(others, chip_peers)
-            ],
-            back.at[pl.ds(0, chips - 1)],
-        )
-        back[chip_at] = pre[chip_at]
-        return handle
-
-    def stage_split(own, par, back, ent, pair, reverse):
+        mine = fresh(2)
+        for (xx, zz), device in zip(others, chip_peers):
+            start(pre.at[xx * nz + zz], back.at[my_shard], device, mine, mine + parity)
+        sent.append((mine, all_others))
+        back[my_shard] = pre[chip_at]
+        return mine
+
+    def stage_split(own, par, back, ent, pair, i, sems, reverse):
+        @pl.when(parity != i)
+        def _():
+            arrived((sems + i, back.at[pl.ds(0, per_head)]))
+
+        @pl.when(parity == i)
+        def _():
+            arrived((sems + i, back.at[pl.ds(0, per_head - 1)]))
+
         one, zero = jnp.ones((1, DH), F32), jnp.zeros((1, DH), F32)
         lead = first(reverse)
-        for i in range(HALF):
-            w_par = jnp.where(lead, decay_row(g_own, i), one)
-            s_par = jnp.where(lead, one, zero)
-            pair[part(i)] = w_par * back[part(i)] + s_par * own[core, part(i)]
-        handle = send([(pair, ent.at[core], partner)], pair)
-        for i in range(HALF):
-            w_own = jnp.where(lead, one, decay_row(g_par, i))
-            s_own = jnp.where(lead, zero, one)
-            ent[core, part(i)] = w_own * back[part(i)] + s_own * par[part(i)]
+        here = pl.ds(i * per_head, per_head)
+        w_par = jnp.where(lead, decay_row(g_own, i), one)
+        s_par = jnp.where(lead, one, zero)
+        pair[part(i)] = w_par * back[part(i)] + s_par * own[core, part(i)]
+        handle = send([(pair.at[here], ent.at[core, here], partner)], pair.at[here])
+        w_own = jnp.where(lead, one, decay_row(g_par, i))
+        s_own = jnp.where(lead, zero, one)
+        ent[core, part(i)] = w_own * back[part(i)] + s_own * par[part(i)]
         return handle
 
     def state_b(ent, h):
@@ -180,25 +213,19 @@
     g_own[...] = jnp.broadcast_to(total, (8, DH))
     ea, tail = jnp.exp(cumul), jnp.exp(total - cumul)
     row_form[0], row_form[1], row_form[2] = cumul, ea, tail
-    pl.semaphore_wait(barrier, len(peers))
-    g_copies = send([(g_own, g_par, partner)], g_par)
-
     loads["k"].wait()
     loads["v"].wait()
-    for h in range(HEADS):
-        weighted = (k[:, lanes(h)].T.astype(F32) * tail[h : h + 1, :]).astype(BF16)
-        f_own[h // HALF, part(h % HALF)] = nn(weighted, v[:, lanes(h)]).reshape(
-            per_head, rows, DH
-        )
-    copies = stage_pair(f_own, f_par)
-    arrived(g_copies)
-    g_all[chip_at] = g_own[...] + g_par[...]
-    g_copies = send(
-        [(g_all.at[chip_at], g_all.at[chip_at], peer) for peer in z_peers],
-        g_all.at[pl.ds(0, nz - 1)],
-    )
-
-    col_form[...] = turned(jnp.concatenate([cumul, ea, tail], axis=0))
+    f_copies = []
+    for i in range(HALF):
+        for h in (i, HALF + i):
+            weighted = (k[:, lanes(h)].T.astype(F32) * tail[h : h + 1, :]).astype(BF16)
+            f_own[h // HALF, part(i)] = nn(weighted, v[:, lanes(h)]).reshape(
+                per_head, rows, DH
+            )
+        if i == 0:
+            pl.semaphore_wait(barrier, len(peers))
+            g_copies = send([(g_own, g_par, partner)], g_par)
+        f_copies.append(stage_pair(f_own, f_par, i))
 
     def column(kind, h):
         j = 8 * kind + h
@@ -240,6 +267,17 @@
         gn[:, lanes(h)] = normed
         gg[:, lanes(h)] = normed * (1.0 - sig)
 
+    arrived(g_copies)
+    g_all[chip_at] = g_own[...] + g_par[...]
+    g_copies = send(
+        [(g_all.at[chip_at], g_all.at[chip_at], peer) for peer in z_peers],
+        g_all.at[pl.ds(0, nz - 1)],
+    )
+    f_sems = fresh()
+    for i in range(HALF):
+        arrived(f_copies[i])
+        stage_chip(f_own, f_par, f_chip, f_zin, i, f_sems, False)
+    col_form[...] = turned(jnp.concatenate([cumul, ea, tail], axis=0))
     loads["q"].wait()
     prepare(0)
     arrived(g_copies)
@@ -248,36 +286,36 @@
         [(g_all.at[row_at], g_all.at[row_at], peer) for peer in x_peers],
         g_all.at[pl.ds(0, nz * (nx - 1))],
     )
-    arrived(copies)
-    copies = stage_chip(f_own, f_par, f_chip, f_zin, False)
     intra(0)
     prepare(1)
     intra(1)
-    prepare(2)
-    intra(2)
     arrived(g_copies)
-    mine = HALF * core + chip_at * rows // DH
     for j in range(chips):
-        decay[j] = jnp.broadcast_to(jnp.exp(g_all[j, pl.ds(mine, 1), :]), (8, DH))
-    arrived(copies)
-    copies = stage_fold(f_zin, f_pre, f_back, False)
-    prepare(3)
-    intra(3)
+        decay[j] = jnp.broadcast_to(
+            jnp.exp(g_all[j, pl.ds(HALF * core + parity, 1), :]), (8, DH)
+        )
+    f_sems = stage_fold(f_zin, f_pre, f_back, f_sems, False)
+    for h in range(2, HEADS):
+        prepare(h)
+        intra(h)
     for name in ("gate", "gout", "gain"):
         loads[name].wait()
     for h in range(HEADS):
         gates(h)
-    arrived(copies)
-    copies = stage_split(f_own, f_par, f_back, f_ent, f_pair, False)
-    arrived(copies)
+    f_copies = [
+        stage_split(f_own, f_par, f_back, f_ent, f_pair, i, f_sems, False)
+        for i in range(HALF)
+    ]
 
     squares = jnp.zeros((BLOCK, DH), F32)
     inner = jnp.zeros((BLOCK, DH), F32)
-    for h in range(HEADS):
-        full = att[:, lanes(h)] + nn(wq[h], state_b(f_ent, h))
-        att[:, lanes(h)] = full
-        squares = squares + full * full
-        inner = inner + full * gn[:, lanes(h)]
+    for i in range(HALF):
+        arrived(f_copies[i])
+        for h in (i, HALF + i):
+            full = att[:, lanes(h)] + nn(wq[h], state_b(f_ent, h))
+            att[:, lanes(h)] = full
+            squares = squares + full * full
+            inner = inner + full * gn[:, lanes(h)]
 
     ones = jnp.ones((8, DH), BF16)
 
@@ -314,11 +352,13 @@
         )
 
     rms_col, coef_col = scale_column(0), scale_column(parts)
-    for h in range(HEADS):
-        grad = (rms_col * gn[:, lanes(h)] - att[:, lanes(h)] * coef_col).astype(BF16)
-        gb[:, lanes(h)] = grad
-        r_own[h // HALF, part(h % HALF)] = nn(wqt[h], grad).reshape(per_head, rows, DH)
-    copies = stage_pair(r_own, r_par)
+    r_copies = []
+    for i in range(HALF):
+        for h in (i, HALF + i):
+            grad = (rms_col * gn[:, lanes(h)] - att[:, lanes(h)] * coef_col).astype(BF16)
+            gb[:, lanes(h)] = grad
+            r_own[h // HALF, part(i)] = nn(wqt[h], grad).reshape(per_head, rows, DH)
+        r_copies.append(stage_pair(r_own, r_par, i))
 
     def back(h):
         grad = gb[:, lanes(h)]
@@ -347,17 +387,21 @@
 
     for h in range(HEADS):
         dg[:, lanes(h)] = (gg[:, lanes(h)] * att[:, lanes(h)] * rms_col).astype(BF16)
-    arrived(copies)
-    copies = stage_chip(r_own, r_par, r_chip, r_zin, True)
+    r_sems = fresh()
+    for i in range(HALF):
+        arrived(r_copies[i])
+        stage_chip(r_own, r_par, r_chip, r_zin, i, r_sems, True)
     back(0)
     back(1)
-    arrived(copies)
-    copies = stage_fold(r_zin, r_pre, r_back, True)
+    r_sems = stage_fold(r_zin, r_pre, r_back, r_sems, True)
     back(2)
     back(3)
-    arrived(copies)
-    copies = stage_split(r_own, r_par, r_back, r_ent, r_pair, True)
-    arrived(copies)
+    r_copies = [
+        stage_split(r_own, r_par, r_back, r_ent, r_pair, i, r_sems, True)
+        for i in range(HALF)
+    ]
+    for i in range(HALF):
+        arrived(r_copies[i])
     for mine, span in sent:
         pltpu.make_async_copy(span, span, send_sem.at[mine]).wait()
 
@@ -410,7 +454,7 @@
         + [halves, shards, shards, shards, shards, shards, shards]
         + [vmem((8, DH)), vmem((nh, 8, DH))]
         + [pltpu.SemaphoreType.DMA((7,))]
-        + [pltpu.SemaphoreType.DMA((12,))] * 2
+        + [pltpu.SemaphoreType.DMA((18,))] * 2
     )
     any_space = pl.BlockSpec(memory_space=pl.ANY)
     in_vmem = pl.BlockSpec(memory_space=pltpu.VMEM)

time: 59 us -> 57.9 us (0.981)
  Pallas kernels: 58.2 us -> 57.1 us
    pallas_call x1, Pallas kernels: 56.8 us -> 55.7 us  [local(): pl.pallas_call(functools.partial(kernel, nx, nz, nh), out_shape=[kept(wid...]
where the time goes in v3:
time: 57.9 us; the launch traced here: 57.8 us
  Pallas kernels  57.1 us (99%)
  between operations  0.64 us (1%)
    pallas_call x1, Pallas kernels, local(): pl.pallas_call(functools.partial(kernel, nx, nz, nh), out_shape=[kept(wid...  55.7 us
    pallas_call x1, Pallas kernels, local(): pl.pallas_call(finish, out_shape=[jax.ShapeDtypeStruct(wide, BF16)] * 4,...  1.39 us

profile of v3, /device:TPU:1, one launch (start us, length us, event | category | flops | bytes accessed | tf_op | source)
XLA Modules:
  0.0 57.8 jit_solution(8592566339513853011)
XLA Ops:
  0.6 55.7 %shard_map.102 = (bf16[512,512]{1,0:T(8,128)(2,1)S(1)}, bf16[512,512]{1,0:T(8,128)(2,1)S(1)}, f32[512,512]{1,0:T(8,128)S(1)}, f32[512,512]{1,0:T(8,128)S(1)}, bf...) custom-call(bf16[512,512]{1,0:T(8,128)(2,1)} %q_hbm.1, ...), custom_call_target="tpu_custom_call" | custom-call | tf_op jit(solution)/shard_map/pallas_call | solution.py:463
  56.4 1.4 %shard_map.103 = (bf16[512,512]{1,0:T(8,128)(2,1)}, bf16[512,512]{1,0:T(8,128)(2,1)}, bf16[512,512]{1,0:T(8,128)(2,1)}, bf16[512,512]{1,0:T(8,128)(2,1)}) custom-call(bf16[512,512]{1,0:T(8,128)(2,1)S(1)} %get-tuple-element.11.dq_in, bf16[512,512]{1,0:T(8,128)(2,1)S(1)} %get-tuple-element.12.dg_in, f32[512,512]{1,0:T(8,128)S(1)} %get-tuple-element.13.dki, ...), custom_call_target="tpu_custom_call" | custom-call | tf_op jit(solution)/shard_map/pallas_call | solution.py:481

commit v4 on v3

--- a/solution.py
+++ b/solution.py
@@ -50,7 +50,7 @@
 
 
 def lanes(h):
-    return slice(h * DH, (h + 1) * DH)
+    return pl.ds(h * DH if isinstance(h, int) else pl.multiple_of(h * DH, DH), DH)
 
 
 def kernel(
@@ -204,8 +204,8 @@
         ent[core, part(i)] = w_own * back[part(i)] + s_own * par[part(i)]
         return handle
 
-    def state_b(ent, h):
-        return ent[h // HALF, part(h % HALF)].reshape(DH, DH).astype(BF16)
+    def state_b(ent, half, i):
+        return ent[half, part(i)].reshape(DH, DH).astype(BF16)
 
     loads["ld"].wait()
     cumul = lane_cumsum(jnp.concatenate([ld[...], ld[...]], axis=0))
@@ -215,17 +215,20 @@
     row_form[0], row_form[1], row_form[2] = cumul, ea, tail
     loads["k"].wait()
     loads["v"].wait()
+    def block_state(half, i):
+        h = HALF * half + i
+        weighted = (k[:, lanes(h)].T.astype(F32) * row_form[2, pl.ds(h, 1), :]).astype(BF16)
+        f_own[half, part(i)] = nn(weighted, v[:, lanes(h)]).reshape(per_head, rows, DH)
+
     f_copies = []
     for i in range(HALF):
-        for h in (i, HALF + i):
-            weighted = (k[:, lanes(h)].T.astype(F32) * tail[h : h + 1, :]).astype(BF16)
-            f_own[h // HALF, part(i)] = nn(weighted, v[:, lanes(h)]).reshape(
-                per_head, rows, DH
-            )
+        block_state(1 - core, i)
         if i == 0:
             pl.semaphore_wait(barrier, len(peers))
             g_copies = send([(g_own, g_par, partner)], g_par)
         f_copies.append(stage_pair(f_own, f_par, i))
+    for i in range(HALF):
+        block_state(core, i)
 
     def column(kind, h):
         j = 8 * kind + h
@@ -267,19 +270,20 @@
         gn[:, lanes(h)] = normed
         gg[:, lanes(h)] = normed * (1.0 - sig)
 
+    col_form[...] = turned(jnp.concatenate([cumul, ea, tail], axis=0))
     arrived(g_copies)
     g_all[chip_at] = g_own[...] + g_par[...]
     g_copies = send(
         [(g_all.at[chip_at], g_all.at[chip_at], peer) for peer in z_peers],
         g_all.at[pl.ds(0, nz - 1)],
     )
+    loads["q"].wait()
+    prepare(0)
     f_sems = fresh()
     for i in range(HALF):
         arrived(f_copies[i])
         stage_chip(f_own, f_par, f_chip, f_zin, i, f_sems, False)
-    col_form[...] = turned(jnp.concatenate([cumul, ea, tail], axis=0))
-    loads["q"].wait()
-    prepare(0)
+    prepare(1)
     arrived(g_copies)
     row_at = pl.ds(x * nz, nz)
     g_copies = send(
@@ -287,7 +291,6 @@
         g_all.at[pl.ds(0, nz * (nx - 1))],
     )
     intra(0)
-    prepare(1)
     intra(1)
     arrived(g_copies)
     for j in range(chips):
@@ -309,10 +312,12 @@
 
     squares = jnp.zeros((BLOCK, DH), F32)
     inner = jnp.zeros((BLOCK, DH), F32)
-    for i in range(HALF):
-        arrived(f_copies[i])
-        for h in (i, HALF + i):
-            full = att[:, lanes(h)] + nn(wq[h], state_b(f_ent, h))
+    for half in (core, 1 - core):
+        for i in range(HALF):
+            if half is not core:
+                arrived(f_copies[i])
+            h = HALF * half + i
+            full = att[:, lanes(h)] + nn(wq[h], state_b(f_ent, half, i))
             att[:, lanes(h)] = full
             squares = squares + full * full
             inner = inner + full * gn[:, lanes(h)]
@@ -353,16 +358,18 @@
 
     rms_col, coef_col = scale_column(0), scale_column(parts)
     r_copies = []
-    for i in range(HALF):
-        for h in (i, HALF + i):
+    for half in (1 - core, core):
+        for i in range(HALF):
+            h = HALF * half + i
             grad = (rms_col * gn[:, lanes(h)] - att[:, lanes(h)] * coef_col).astype(BF16)
             gb[:, lanes(h)] = grad
-            r_own[h // HALF, part(i)] = nn(wqt[h], grad).reshape(per_head, rows, DH)
-        r_copies.append(stage_pair(r_own, r_par, i))
+            r_own[half, part(i)] = nn(wqt[h], grad).reshape(per_head, rows, DH)
+            if half is not core:
+                r_copies.append(stage_pair(r_own, r_par, i))
 
     def back(h):
         grad = gb[:, lanes(h)]
-        entering = state_b(f_ent, h)
+        entering = state_b(f_ent, h // HALF, h % HALF)
         upper = []
         for t in range(0, BLOCK, TILE):
             seen = t + TILE

time: 57.9 us -> 57.6 us (level)
  no operation moved by 1% of the time
where the time goes in v4:
time: 57.6 us; the launch traced here: 57.4 us
  Pallas kernels  56.8 us (99%)
  between operations  0.64 us (1%)
    pallas_call x1, Pallas kernels, local(): pl.pallas_call(functools.partial(kernel, nx, nz, nh), out_shape=[kept(wid...  55.4 us
    pallas_call x1, Pallas kernels, local(): pl.pallas_call(finish, out_shape=[jax.ShapeDtypeStruct(wide, BF16)] * 4,...  1.39 us

profile of v4, /device:TPU:1, one launch (start us, length us, event | category | flops | bytes accessed | tf_op | source)
XLA Modules:
  0.0 57.4 jit_solution(13010212261829733342)
XLA Ops:
  0.6 55.4 %shard_map.102 = (bf16[512,512]{1,0:T(8,128)(2,1)S(1)}, bf16[512,512]{1,0:T(8,128)(2,1)S(1)}, f32[512,512]{1,0:T(8,128)S(1)}, f32[512,512]{1,0:T(8,128)S(1)}, bf...) custom-call(bf16[512,512]{1,0:T(8,128)(2,1)} %q_hbm.1, ...), custom_call_target="tpu_custom_call" | custom-call | tf_op jit(solution)/shard_map/pallas_call | solution.py:470
  56.0 1.4 %shard_map.103 = (bf16[512,512]{1,0:T(8,128)(2,1)}, bf16[512,512]{1,0:T(8,128)(2,1)}, bf16[512,512]{1,0:T(8,128)(2,1)}, bf16[512,512]{1,0:T(8,128)(2,1)}) custom-call(bf16[512,512]{1,0:T(8,128)(2,1)S(1)} %get-tuple-element.11.dq_in, bf16[512,512]{1,0:T(8,128)(2,1)S(1)} %get-tuple-element.12.dg_in, f32[512,512]{1,0:T(8,128)S(1)} %get-tuple-element.13.dki, ...), custom_call_target="tpu_custom_call" | custom-call | tf_op jit(solution)/shard_map/pallas_call | solution.py:488

commit v5 on v4

--- a/solution.py
+++ b/solution.py
@@ -58,9 +58,9 @@
     q_hbm, k_hbm, v_hbm, gate_hbm, gout_hbm, ld_hbm, gain_hbm,
     dq, dg, dki, dvi, wk, wv, r_ent,
     q, k, v, gate, gout, ld, gain,
-    row_form, col_form, ea_col,
+    row_form, col_form, columns,
     qt, wqt, wq, mask, fw, att, gn, gg, gb,
-    g_own, g_par, g_all, decay,
+    g_own, g_par, g_all, decay, x_out, x_in, att_par, wqt_par,
     f_own, f_par, f_chip, f_zin, f_back, f_ent, f_pair, f_pre,
     r_own, r_par, r_chip, r_zin, r_back, r_pair, r_pre,
     y_out, y_in,
@@ -90,7 +90,12 @@
     z_peers = [at(x, (z + d) % nz, core) for d in range(1, nz)]
     x_peers = [at((x + d) % nx, z, core) for d in range(1, nx)]
     chip_peers = [at(xx, zz, core) for xx, zz in others]
-    y_peers = [(me, shifted(head, d, nh)) for d in outward(nh) if d]
+    y_peers = [
+        (at(x, z, c)[0], shifted(head, d, nh))
+        for d in outward(nh)
+        for c in (core, 1 - core)
+        if d
+    ]
 
     loads = {}
     for i, (name, src, dst) in enumerate((
@@ -230,25 +235,26 @@
     for i in range(HALF):
         block_state(core, i)
 
-    def column(kind, h):
-        j = 8 * kind + h
-        return jnp.broadcast_to(col_form[:, j : j + 1], (BLOCK, DH))
+    def spread():
+        for kind in range(3):
+            for h in range(HEADS):
+                j = 8 * kind + h
+                columns[kind, h] = jnp.broadcast_to(col_form[:, j : j + 1], (BLOCK, DH))
 
     def prepare(h):
-        ea_here = column(1, h)
-        tail_here = column(2, h)
-        ea_col[h] = ea_here
+        ea_here = columns[1, h]
+        tail_here = columns[2, h]
         q_here = q[:, lanes(h)]
         wq[h] = (q_here.astype(F32) * ea_here).astype(BF16)
         wk[:, lanes(h)] = (k[:, lanes(h)].astype(F32) * tail_here).astype(BF16)
         wv[:, lanes(h)] = (v[:, lanes(h)].astype(F32) * tail_here).astype(BF16)
         turned_q = q_here.T
         qt[h] = turned_q
-        wqt[h] = (turned_q.astype(F32) * row_form[1, h : h + 1, :]).astype(BF16)
+        wqt[h] = (turned_q.astype(F32) * row_form[1, pl.ds(h, 1), :]).astype(BF16)
 
     def intra(h):
-        a_here = row_form[0, h : h + 1, :]
-        a_col = column(0, h)
+        a_here = row_form[0, pl.ds(h, 1), :]
+        a_col = columns[0, h]
         for t in range(0, BLOCK, TILE):
             seen = t + TILE
             here = slice(t, seen)
@@ -277,50 +283,64 @@
         [(g_all.at[chip_at], g_all.at[chip_at], peer) for peer in z_peers],
         g_all.at[pl.ds(0, nz - 1)],
     )
-    loads["q"].wait()
-    prepare(0)
+    spread()
     f_sems = fresh()
     for i in range(HALF):
         arrived(f_copies[i])
         stage_chip(f_own, f_par, f_chip, f_zin, i, f_sems, False)
-    prepare(1)
     arrived(g_copies)
     row_at = pl.ds(x * nz, nz)
     g_copies = send(
         [(g_all.at[row_at], g_all.at[row_at], peer) for peer in x_peers],
         g_all.at[pl.ds(0, nz * (nx - 1))],
     )
-    intra(0)
-    intra(1)
+    for name in ("q", "gate", "gout", "gain"):
+        loads[name].wait()
+    for i in range(HALF):
+        h = HALF * (1 - core) + i
+        prepare(h)
+        intra(h)
+        gates(h)
+        x_out[0, i] = wq[h].astype(F32)
+        x_out[1, i] = att[:, lanes(h)]
+        x_out[2, i] = gn[:, lanes(h)]
+    x_copies = send([(x_out, x_in, partner)], x_in)
     arrived(g_copies)
     for j in range(chips):
         decay[j] = jnp.broadcast_to(
             jnp.exp(g_all[j, pl.ds(HALF * core + parity, 1), :]), (8, DH)
         )
     f_sems = stage_fold(f_zin, f_pre, f_back, f_sems, False)
-    for h in range(2, HEADS):
+    for i in range(HALF):
+        h = HALF * core + i
         prepare(h)
         intra(h)
-    for name in ("gate", "gout", "gain"):
-        loads[name].wait()
-    for h in range(HEADS):
         gates(h)
-    f_copies = [
-        stage_split(f_own, f_par, f_back, f_ent, f_pair, i, f_sems, False)
-        for i in range(HALF)
-    ]
-
-    squares = jnp.zeros((BLOCK, DH), F32)
-    inner = jnp.zeros((BLOCK, DH), F32)
-    for half in (core, 1 - core):
-        for i in range(HALF):
-            if half is not core:
-                arrived(f_copies[i])
-            h = HALF * half + i
-            full = att[:, lanes(h)] + nn(wq[h], state_b(f_ent, half, i))
-            att[:, lanes(h)] = full
-            squares = squares + full * full
-            inner = inner + full * gn[:, lanes(h)]
+    arrived(x_copies)
+    for i in range(HALF):
+        wqt_par[i] = x_in[0, i].T.astype(BF16)
+
+    def attend(h, entering):
+        full = att[:, lanes(h)] + nn(wq[h], entering)
+        att[:, lanes(h)] = full
+        return full
+
+    none = jnp.zeros((BLOCK, DH), F32)
+    squares, inner, squares_par, inner_par = none, none, none, none
+    f_copies = []
+    for i in range(HALF):
+        f_copies.append(
+            stage_split(f_own, f_par, f_back, f_ent, f_pair, i, f_sems, False)
+        )
+        h = HALF * core + i
+        full = attend(h, state_b(f_ent, core, i))
+        squares = squares + full * full
+        inner = inner + full * gn[:, lanes(h)]
+        entering_par = f_pair[part(i)].reshape(DH, DH).astype(BF16)
+        full = x_in[1, i] + nn(x_in[0, i].astype(BF16), entering_par)
+        att_par[i] = full
+        squares_par = squares_par + full * full
+        inner_par = inner_par + full * x_in[2, i]
 
     ones = jnp.ones((8, DH), BF16)
 
@@ -329,23 +349,33 @@
         low = (value - high.astype(F32)).astype(BF16)
         return nt(ones, high) + nt(ones, low)
 
-    sums = [row_sums(squares), row_sums(inner)]
     parts = BLOCK // DH
-    y_out[...] = jnp.concatenate(
-        [s[0:1, i * DH : (i + 1) * DH] for s in sums for i in range(parts)], axis=0
+
+    def tile(*values):
+        sums = [row_sums(value) for value in values]
+        return jnp.concatenate(
+            [s[0:1, i * DH : (i + 1) * DH] for s in sums for i in range(parts)], axis=0
+        )
+
+    y_out[core] = tile(squares, inner)
+    y_out[1 - core] = tile(squares_par, inner_par)
+    slot = 2 * head + core
+    copies = send(
+        [(y_out, y_in.at[slot], peer) for peer in y_peers + [partner]],
+        y_in.at[pl.ds(0, 2 * nh - 1)],
     )
-    copies = send(
-        [(y_out, y_in.at[head], peer) for peer in y_peers], y_in.at[pl.ds(0, nh - 1)]
-    )
-    y_in[head] = y_out[...]
+    y_in[slot] = y_out[...]
     arrived(copies)
-    summed = y_in[0]
-    for i in range(1, nh):
-        summed = summed + y_in[i]
     features = HEADS * DH * nh
-    rms = lax.rsqrt(summed[:parts] / features + 1e-05)
-    coef = rms * rms * rms * summed[parts:] / features
-    scales = turned(jnp.concatenate([rms, coef], axis=0))
+
+    def row_scales(block):
+        summed = y_in[0, block]
+        for i in range(1, 2 * nh):
+            summed = summed + y_in[i, block]
+        rms = lax.rsqrt(summed[:parts] / features + 1e-05)
+        return [rms, rms * rms * rms * summed[parts:] / features]
+
+    scales = turned(jnp.concatenate(row_scales(core) + row_scales(1 - core), axis=0))
 
     def scale_column(first_lane):
         return jnp.concatenate(
@@ -357,15 +387,25 @@
         )
 
     rms_col, coef_col = scale_column(0), scale_column(parts)
-    r_copies = []
-    for half in (1 - core, core):
-        for i in range(HALF):
-            h = HALF * half + i
-            grad = (rms_col * gn[:, lanes(h)] - att[:, lanes(h)] * coef_col).astype(BF16)
-            gb[:, lanes(h)] = grad
-            r_own[half, part(i)] = nn(wqt[h], grad).reshape(per_head, rows, DH)
-            if half is not core:
-                r_copies.append(stage_pair(r_own, r_par, i))
+    rms_par, coef_par = scale_column(2 * parts), scale_column(3 * parts)
+
+    def gradient(h):
+        grad = (rms_col * gn[:, lanes(h)] - att[:, lanes(h)] * coef_col).astype(BF16)
+        gb[:, lanes(h)] = grad
+        return grad
+
+    r_sems = fresh()
+    for i in range(HALF):
+        h = HALF * core + i
+        r_own[core, part(i)] = nn(wqt[h], gradient(h)).reshape(per_head, rows, DH)
+        grad = (rms_par * x_in[2, i] - att_par[i] * coef_par).astype(BF16)
+        r_par[part(i)] = nn(wqt_par[i], grad).reshape(per_head, rows, DH)
+        stage_chip(r_own, r_par, r_chip, r_zin, i, r_sems, True)
+    for i in range(HALF):
+        h = HALF * (1 - core) + i
+        arrived(f_copies[i])
+        attend(h, state_b(f_ent, 1 - core, i))
+        gradient(h)
 
     def back(h):
         grad = gb[:, lanes(h)]
@@ -377,7 +417,7 @@
             weights = (nt(grad[here], v[:seen, lanes(h)]) * mask[h, here, :seen]).astype(BF16)
             upper.append(weights)
             dq[here, lanes(h)] = (
-                nn(weights, k[:seen, lanes(h)]) + ea_col[h, here, :] * nt(grad[here], entering)
+                nn(weights, k[:seen, lanes(h)]) + columns[1, h, here, :] * nt(grad[here], entering)
             ).astype(BF16)
         gt = grad.T
         for s in range(0, BLOCK, TILE):
@@ -394,10 +434,6 @@
 
     for h in range(HEADS):
         dg[:, lanes(h)] = (gg[:, lanes(h)] * att[:, lanes(h)] * rms_col).astype(BF16)
-    r_sems = fresh()
-    for i in range(HALF):
-        arrived(r_copies[i])
-        stage_chip(r_own, r_par, r_chip, r_zin, i, r_sems, True)
     back(0)
     back(1)
     r_sems = stage_fold(r_zin, r_pre, r_back, r_sems, True)
@@ -449,7 +485,7 @@
     scratch = (
         [vmem(wide, BF16)] * 5
         + [vmem((HEADS, BLOCK)), vmem((1, HEADS * DH))]
-        + [vmem((3, 8, BLOCK)), vmem((BLOCK, DH)), vmem(per_head)]
+        + [vmem((3, 8, BLOCK)), vmem((BLOCK, DH)), vmem((3,) + per_head)]
         + [vmem((HEADS, DH, BLOCK), BF16)] * 2
         + [vmem(per_head, BF16)]
         + [vmem((HEADS, BLOCK, BLOCK)), vmem((HEADS, BLOCK, BLOCK), BF16)]
@@ -457,11 +493,13 @@
         + [vmem(wide, BF16)]
         + [vmem((8, DH))] * 2
         + [vmem((chips, 8, DH))] * 2
+        + [vmem((3, HALF, BLOCK, DH))] * 2
+        + [vmem((HALF, BLOCK, DH)), vmem((HALF, DH, BLOCK), BF16)]
         + [halves, shards, shards, shards, shards, halves, shards, shards]
         + [halves, shards, shards, shards, shards, shards, shards]
-        + [vmem((8, DH)), vmem((nh, 8, DH))]
+        + [vmem((2, 8, DH)), vmem((2 * nh, 2, 8, DH))]
         + [pltpu.SemaphoreType.DMA((7,))]
-        + [pltpu.SemaphoreType.DMA((18,))] * 2
+        + [pltpu.SemaphoreType.DMA((17,))] * 2
     )
     any_space = pl.BlockSpec(memory_space=pl.ANY)
     in_vmem = pl.BlockSpec(memory_space=pltpu.VMEM)

time: 57.6 us -> 56.2 us (0.976)
  Pallas kernels: 56.8 us -> 55.4 us
    pallas_call x1, Pallas kernels: 55.4 us -> 54 us  [local(): pl.pallas_call(functools.partial(kernel, nx, nz, nh), out_shape=[kept(wid...]
where the time goes in v5:
time: 56.2 us; the launch traced here: 56 us
  Pallas kernels  55.4 us (99%)
  between operations  0.64 us (1%)
    pallas_call x1, Pallas kernels, local(): pl.pallas_call(functools.partial(kernel, nx, nz, nh), out_shape=[kept(wid...  54 us
    pallas_call x1, Pallas kernels, local(): pl.pallas_call(finish, out_shape=[jax.ShapeDtypeStruct(wide, BF16)] * 4,...  1.39 us

profile of v5, /device:TPU:1, one launch (start us, length us, event | category | flops | bytes accessed | tf_op | source)
XLA Modules:
  0.0 56.0 jit_solution(1166124376511864335)
XLA Ops:
  0.6 54.0 %shard_map.102 = (bf16[512,512]{1,0:T(8,128)(2,1)S(1)}, bf16[512,512]{1,0:T(8,128)(2,1)S(1)}, f32[512,512]{1,0:T(8,128)S(1)}, f32[512,512]{1,0:T(8,128)S(1)}, bf...) custom-call(bf16[512,512]{1,0:T(8,128)(2,1)} %q_hbm.1, ...), custom_call_target="tpu_custom_call" | custom-call | tf_op jit(solution)/shard_map/pallas_call | solution.py:508
  54.6 1.4 %shard_map.103 = (bf16[512,512]{1,0:T(8,128)(2,1)}, bf16[512,512]{1,0:T(8,128)(2,1)}, bf16[512,512]{1,0:T(8,128)(2,1)}, bf16[512,512]{1,0:T(8,128)(2,1)}) custom-call(bf16[512,512]{1,0:T(8,128)(2,1)S(1)} %get-tuple-element.11.dq_in, bf16[512,512]{1,0:T(8,128)(2,1)S(1)} %get-tuple-element.12.dg_in, f32[512,512]{1,0:T(8,128)S(1)} %get-tuple-element.13.dki, ...), custom_call_target="tpu_custom_call" | custom-call | tf_op jit(solution)/shard_map/pallas_call | solution.py:526

commit v6 on v5

--- a/solution.py
+++ b/solution.py
@@ -56,11 +56,11 @@
 def kernel(
     nx, nz, nh,
     q_hbm, k_hbm, v_hbm, gate_hbm, gout_hbm, ld_hbm, gain_hbm,
-    dq, dg, dki, dvi, wk, wv, r_ent,
+    dq, dg, dk, dv, dki, dvi, wk, wv, r_ent,
     q, k, v, gate, gout, ld, gain,
     row_form, col_form, columns,
     qt, wqt, wq, mask, fw, att, gn, gg, gb,
-    g_own, g_par, g_all, decay, x_out, x_in, att_par, wqt_par,
+    g_own, g_par, g_all, decay, x_out, x_in, att_par, wq_par, wqt_par,
     f_own, f_par, f_chip, f_zin, f_back, f_ent, f_pair, f_pre,
     r_own, r_par, r_chip, r_zin, r_back, r_pair, r_pre,
     y_out, y_in,
@@ -296,15 +296,16 @@
     )
     for name in ("q", "gate", "gout", "gain"):
         loads[name].wait()
+    x_copies = []
     for i in range(HALF):
         h = HALF * (1 - core) + i
         prepare(h)
         intra(h)
         gates(h)
-        x_out[0, i] = wq[h].astype(F32)
-        x_out[1, i] = att[:, lanes(h)]
-        x_out[2, i] = gn[:, lanes(h)]
-    x_copies = send([(x_out, x_in, partner)], x_in)
+        x_out[i, 0] = wq[h].astype(F32)
+        x_out[i, 1] = att[:, lanes(h)]
+        x_out[i, 2] = gn[:, lanes(h)]
+        x_copies.append(send([(x_out.at[i], x_in.at[i], partner)], x_in.at[i]))
     arrived(g_copies)
     for j in range(chips):
         decay[j] = jnp.broadcast_to(
@@ -316,9 +317,10 @@
         prepare(h)
         intra(h)
         gates(h)
-    arrived(x_copies)
-    for i in range(HALF):
-        wqt_par[i] = x_in[0, i].T.astype(BF16)
+    for i in range(HALF):
+        arrived(x_copies[i])
+        wq_par[i] = x_in[i, 0].astype(BF16)
+        wqt_par[i] = x_in[i, 0].T.astype(BF16)
 
     def attend(h, entering):
         full = att[:, lanes(h)] + nn(wq[h], entering)
@@ -337,17 +339,15 @@
         squares = squares + full * full
         inner = inner + full * gn[:, lanes(h)]
         entering_par = f_pair[part(i)].reshape(DH, DH).astype(BF16)
-        full = x_in[1, i] + nn(x_in[0, i].astype(BF16), entering_par)
+        full = x_in[i, 1] + nn(wq_par[i], entering_par)
         att_par[i] = full
         squares_par = squares_par + full * full
-        inner_par = inner_par + full * x_in[2, i]
+        inner_par = inner_par + full * x_in[i, 2]
 
     ones = jnp.ones((8, DH), BF16)
 
     def row_sums(value):
-        high = value.astype(BF16)
-        low = (value - high.astype(F32)).astype(BF16)
-        return nt(ones, high) + nt(ones, low)
+        return nt(ones, value.astype(BF16))
 
     parts = BLOCK // DH
 
@@ -398,7 +398,7 @@
     for i in range(HALF):
         h = HALF * core + i
         r_own[core, part(i)] = nn(wqt[h], gradient(h)).reshape(per_head, rows, DH)
-        grad = (rms_par * x_in[2, i] - att_par[i] * coef_par).astype(BF16)
+        grad = (rms_par * x_in[i, 2] - att_par[i] * coef_par).astype(BF16)
         r_par[part(i)] = nn(wqt_par[i], grad).reshape(per_head, rows, DH)
         stage_chip(r_own, r_par, r_chip, r_zin, i, r_sems, True)
     for i in range(HALF):
@@ -444,30 +444,40 @@
         for i in range(HALF)
     ]
     for i in range(HALF):
+        here = lanes(HALF * core + i)
+        leaving = state_b(r_ent, core, i)
+        dk[:, here] = (dki[:, here] + nt(wv[:, here], leaving)).astype(BF16)
+        dv[:, here] = (dvi[:, here] + nn(wk[:, here], leaving)).astype(BF16)
+    for i in range(HALF):
         arrived(r_copies[i])
     for mine, span in sent:
         pltpu.make_async_copy(span, span, send_sem.at[mine]).wait()
 
 
 def finish(
-    dq_in, dg_in, dki, dvi, wk, wv, ent, dq_hbm, dk_hbm, dv_hbm, dg_hbm, dk, dv, sem
+    dq_in, dg_in, dk_in, dv_in, dki, dvi, wk, wv, ent,
+    dq_hbm, dk_hbm, dv_hbm, dg_hbm, dk, dv, sem,
 ):
-    copies = [
-        pltpu.make_async_copy(dq_in, dq_hbm, sem.at[0]),
-        pltpu.make_async_copy(dg_in, dg_hbm, sem.at[1]),
-    ]
-    for copy in copies:
+    core = lax.axis_index("ctx") % 2
+    copies = []
+
+    def store(src, dst):
+        copy = pltpu.make_async_copy(src, dst, sem.at[len(copies)])
         copy.start()
-    for h in range(HEADS):
+        copies.append(copy)
+
+    store(dq_in, dq_hbm)
+    store(dg_in, dg_hbm)
+    mine = pl.ds(pl.multiple_of(core * HALF * DH, DH), HALF * DH)
+    store(dk_in.at[:, mine], dk_hbm.at[:, mine])
+    store(dv_in.at[:, mine], dv_hbm.at[:, mine])
+    for i in range(HALF):
+        h = HALF * (1 - core) + i
         leaving = ent[h].astype(BF16)
-        dk[:, lanes(h)] = (dki[:, lanes(h)] + nt(wv[:, lanes(h)], leaving)).astype(BF16)
-        dv[:, lanes(h)] = (dvi[:, lanes(h)] + nn(wk[:, lanes(h)], leaving)).astype(BF16)
-        for i, (src, dst) in enumerate(((dk, dk_hbm), (dv, dv_hbm))):
-            copy = pltpu.make_async_copy(
-                src.at[:, lanes(h)], dst.at[:, lanes(h)], sem.at[2 + 2 * h + i]
-            )
-            copy.start()
-            copies.append(copy)
+        dk[i] = (dki[:, lanes(h)] + nt(wv[:, lanes(h)], leaving)).astype(BF16)
+        store(dk.at[i], dk_hbm.at[:, lanes(h)])
+        dv[i] = (dvi[:, lanes(h)] + nn(wk[:, lanes(h)], leaving)).astype(BF16)
+        store(dv.at[i], dv_hbm.at[:, lanes(h)])
     for copy in copies:
         copy.wait()
 
@@ -493,13 +503,14 @@
         + [vmem(wide, BF16)]
         + [vmem((8, DH))] * 2
         + [vmem((chips, 8, DH))] * 2
-        + [vmem((3, HALF, BLOCK, DH))] * 2
-        + [vmem((HALF, BLOCK, DH)), vmem((HALF, DH, BLOCK), BF16)]
+        + [vmem((HALF, 3, BLOCK, DH))] * 2
+        + [vmem((HALF, BLOCK, DH)), vmem((HALF, BLOCK, DH), BF16)]
+        + [vmem((HALF, DH, BLOCK), BF16)]
         + [halves, shards, shards, shards, shards, halves, shards, shards]
         + [halves, shards, shards, shards, shards, shards, shards]
         + [vmem((2, 8, DH)), vmem((2 * nh, 2, 8, DH))]
         + [pltpu.SemaphoreType.DMA((7,))]
-        + [pltpu.SemaphoreType.DMA((17,))] * 2
+        + [pltpu.SemaphoreType.DMA((18,))] * 2
     )
     any_space = pl.BlockSpec(memory_space=pl.ANY)
     in_vmem = pl.BlockSpec(memory_space=pltpu.VMEM)
@@ -507,12 +518,12 @@
     def local(q, k, v, gate, gout, log_decay, gain):
         made = pl.pallas_call(
             functools.partial(kernel, nx, nz, nh),
-            out_shape=[kept(wide, BF16)] * 2
+            out_shape=[kept(wide, BF16)] * 4
             + [kept(wide, F32)] * 2
             + [kept(wide, BF16)] * 2
             + [kept((HALF, chips, rows, DH), F32)],
             in_specs=[any_space] * 7,
-            out_specs=[in_vmem] * 7,
+            out_specs=[in_vmem] * 9,
             scratch_shapes=scratch,
             compiler_params=pltpu.CompilerParams(
                 collective_id=0, has_side_effects=True, vmem_limit_bytes=36 * 2**20
@@ -526,9 +537,10 @@
             pl.pallas_call(
                 finish,
                 out_shape=[jax.ShapeDtypeStruct(wide, BF16)] * 4,
-                in_specs=[in_vmem] * 7,
+                in_specs=[in_vmem] * 9,
                 out_specs=[any_space] * 4,
-                scratch_shapes=[vmem(wide, BF16)] * 2 + [pltpu.SemaphoreType.DMA((10,))],
+                scratch_shapes=[vmem((HALF, BLOCK, DH), BF16)] * 2
+                + [pltpu.SemaphoreType.DMA((8,))],
                 compiler_params=pltpu.CompilerParams(vmem_limit_bytes=8 * 2**20),
             )(*placed(made, pltpu.VMEM))
         )

time: 56.2 us -> 56 us (level)
  no operation moved by 1% of the time
where the time goes in v6:
time: 56 us; the launch traced here: 55.9 us
  Pallas kernels  55.2 us (99%)
  between operations  0.64 us (1%)
    pallas_call x1, Pallas kernels, local(): pl.pallas_call(functools.partial(kernel, nx, nz, nh), out_shape=[kept(wid...  53.9 us
    pallas_call x1, Pallas kernels, local(): pl.pallas_call(finish, out_shape=[jax.ShapeDtypeStruct(wide, BF16)] * 4,...  1.39 us

profile of v6, /device:TPU:1, one launch (start us, length us, event | category | flops | bytes accessed | tf_op | source)
XLA Modules:
  0.0 55.9 jit_solution(8843893374217802667)
XLA Ops:
  0.6 53.9 %shard_map.102 = (bf16[512,512]{1,0:T(8,128)(2,1)S(1)}, bf16[512,512]{1,0:T(8,128)(2,1)S(1)}, bf16[512,512]{1,0:T(8,128)(2,1)S(1)}, bf16[512,512]{1,0:T(8,128)(2...) custom-call(bf16[512,512]{1,0:T(8,128)(2,1)} %q_hbm.1, ...), custom_call_target="tpu_custom_call" | custom-call | tf_op jit(solution)/shard_map/pallas_call | solution.py:519
  54.5 1.4 %shard_map.103 = (bf16[512,512]{1,0:T(8,128)(2,1)}, bf16[512,512]{1,0:T(8,128)(2,1)}, bf16[512,512]{1,0:T(8,128)(2,1)}, bf16[512,512]{1,0:T(8,128)(2,1)}) custom-call(bf16[512,512]{1,0:T(8,128)(2,1)S(1)} %get-tuple-element.13.dq_in, bf16[512,512]{1,0:T(8,128)(2,1)S(1)} %get-tuple-element.14.dg_in, bf16[512,512]{1,0:T(8,128)(2,1)S(1)} %get-tuple-element.15.dk_in, ...), custom_call_target="tpu_custom_call" | custom-call | tf_op jit(solution)/shard_map/pallas_call | solution.py:537

commit v7 on v6

--- a/solution.py
+++ b/solution.py
@@ -435,8 +435,8 @@
     for h in range(HEADS):
         dg[:, lanes(h)] = (gg[:, lanes(h)] * att[:, lanes(h)] * rms_col).astype(BF16)
     back(0)
+    r_sems = stage_fold(r_zin, r_pre, r_back, r_sems, True)
     back(1)
-    r_sems = stage_fold(r_zin, r_pre, r_back, r_sems, True)
     back(2)
     back(3)
     r_copies = [
@@ -463,11 +463,13 @@
 
     def store(src, dst):
         copy = pltpu.make_async_copy(src, dst, sem.at[len(copies)])
-        copy.start()
+        copy.start(priority=len(copies) % 2)
         copies.append(copy)
 
-    store(dq_in, dq_hbm)
-    store(dg_in, dg_hbm)
+    for first in range(0, BLOCK, TILE):
+        here = pl.ds(first, TILE)
+        store(dq_in.at[here], dq_hbm.at[here])
+        store(dg_in.at[here], dg_hbm.at[here])
     mine = pl.ds(pl.multiple_of(core * HALF * DH, DH), HALF * DH)
     store(dk_in.at[:, mine], dk_hbm.at[:, mine])
     store(dv_in.at[:, mine], dv_hbm.at[:, mine])
@@ -540,7 +542,7 @@
                 in_specs=[in_vmem] * 9,
                 out_specs=[any_space] * 4,
                 scratch_shapes=[vmem((HALF, BLOCK, DH), BF16)] * 2
-                + [pltpu.SemaphoreType.DMA((8,))],
+                + [pltpu.SemaphoreType.DMA((10,))],
                 compiler_params=pltpu.CompilerParams(vmem_limit_bytes=8 * 2**20),
             )(*placed(made, pltpu.VMEM))
         )

time: 56 us -> 56.2 us (level)
  no operation moved by 1% of the time
where the time goes in v7:
time: 56.2 us; the launch traced here: 56 us
  Pallas kernels  55.4 us (99%)
  between operations  0.64 us (1%)
    pallas_call x1, Pallas kernels, local(): pl.pallas_call(functools.partial(kernel, nx, nz, nh), out_shape=[kept(wid...  53.9 us
    pallas_call x1, Pallas kernels, local(): pl.pallas_call(finish, out_shape=[jax.ShapeDtypeStruct(wide, BF16)] * 4,...  1.51 us

profile of v7, /device:TPU:1, one launch (start us, length us, event | category | flops | bytes accessed | tf_op | source)
XLA Modules:
  0.0 56.0 jit_solution(14941062173921344784)
XLA Ops:
  0.6 53.9 %shard_map.102 = (bf16[512,512]{1,0:T(8,128)(2,1)S(1)}, bf16[512,512]{1,0:T(8,128)(2,1)S(1)}, bf16[512,512]{1,0:T(8,128)(2,1)S(1)}, bf16[512,512]{1,0:T(8,128)(2...) custom-call(bf16[512,512]{1,0:T(8,128)(2,1)} %q_hbm.1, ...), custom_call_target="tpu_custom_call" | custom-call | tf_op jit(solution)/shard_map/pallas_call | solution.py:521
  54.5 1.5 %shard_map.103 = (bf16[512,512]{1,0:T(8,128)(2,1)}, bf16[512,512]{1,0:T(8,128)(2,1)}, bf16[512,512]{1,0:T(8,128)(2,1)}, bf16[512,512]{1,0:T(8,128)(2,1)}) custom-call(bf16[512,512]{1,0:T(8,128)(2,1)S(1)} %get-tuple-element.13.dq_in, bf16[512,512]{1,0:T(8,128)(2,1)S(1)} %get-tuple-element.14.dg_in, bf16[512,512]{1,0:T(8,128)(2,1)S(1)} %get-tuple-element.15.dk_in, ...), custom_call_target="tpu_custom_call" | custom-call | tf_op jit(solution)/shard_map/pallas_call | solution.py:539
